TPU v7x, 256 devices: a whole 4x4x8 slice. The times are simulated.
256 devices in a mesh: pipe: 2 (over core), dp: 128 (over z, y, x).
Axes of the slice: x: 4, y: 4, z: 8, core: 2. Of those that a mesh axis runs over, the one named last changes fastest.
Arguments:
- tiles: bfloat16 [2, 128, 16, 8, 2048], P(None, 'dp'), may hold values from -6 to 6
- counts: int32 [2, 128], P(None, 'dp'), may hold values from 1 to 16, 512 in all within a row
- cells: int32 [2, 128, 16], P(None, 'dp'), may hold values from 0 to 255, as said below
- block_in: bfloat16 [2, 2048, 512], P('pipe'), may hold values from -0.125 to 0.125
- block_out: bfloat16 [2, 512, 2048], P('pipe'), may hold values from -0.25 to 0.25
- proj: bfloat16 [2048, 1536], P(None, 'pipe'), may hold values from -0.125 to 0.125
- depth: float32 [2, 9, 1536], P(None, None, 'pipe'), may hold values from -2 to 2
- point: bfloat16 [2, 1536, 1536], P(None, 'pipe'), may hold values from -0.15625 to 0.15625
- bias: float32 [2, 1536], P(None, 'pipe'), may hold values from -3 to 3
- cotangent: bfloat16 [2, 128, 256, 1536], P(None, 'dp', None, 'pipe'), may hold values from -6 to 6
Outputs:
- mixed: bfloat16 [2, 128, 256, 1536], P(None, 'dp', None, 'pipe')
- grad_proj: float32 [2048, 1536], P('dp', 'pipe')
- grad_point: float32 [2, 1536, 1536], P(None, 'pipe', 'dp')
- grad_depth: float32 [2, 9, 1536], P(None, None, 'pipe')
- grad_bias: float32 [2, 1536], P(None, 'pipe')
Inputs may be any that keep to these rules, and one draw needn't show every extreme that they name: In each micro-batch the counts of the 128 slides sum to 512, and the largest is exactly 16. The 16 cells of one slide in one micro-batch are distinct.
All inputs are finite; a program needn't handle non-finite values. No bound on the sum of `counts` on one device may be relied on, other than what follows from the above.
Results may differ from a plain program's by a relative error of at most 0.02.
Values may be sent and summed in bfloat16 or wider, within the bound.
No kernel may reach another device: no remote copies, remote signals or barrier semaphores. Data moves between devices by JAX's collectives and lax.ppermute only.
A program may use at most 128 MiB of HBM per device.

v0:
```python
import jax
import jax.numpy as jnp
from jax import lax
from jax.sharding import PartitionSpec as P

LAYERS = 2
GH = 16
GW = 16


def passed_along(value, axis, steps):
    count = lax.axis_size(axis)
    first, last = (max(0, -steps), min(count, count - steps))
    return lax.ppermute(value, axis, [(source, source + steps) for source in range(first, last)])


def broadcast(block, axis, holder):
    block = jnp.where(lax.axis_index(axis) == holder, block, jnp.zeros_like(block))
    return lax.psum(block, axis)


def encode_block(row_block, w_in, w_out):
    hidden = jnp.maximum(jnp.dot(row_block, w_in, preferred_element_type=jnp.float32), 0.0).astype(
        jnp.bfloat16
    )
    summed = row_block.astype(jnp.float32) + jnp.dot(
        hidden, w_out, preferred_element_type=jnp.float32
    )
    return jnp.maximum(summed, 0.0).astype(jnp.bfloat16)


def dilated(field_f, kernel, dilation):
    height, breadth = (field_f.shape[1], field_f.shape[2])
    padded = jnp.pad(field_f, ((0, 0), (dilation, dilation), (dilation, dilation), (0, 0)))
    result = jnp.zeros_like(field_f)
    for row_off in range(3):
        for col_off in range(3):
            taps = padded[
                :,
                row_off * dilation : row_off * dilation + height,
                col_off * dilation : col_off * dilation + breadth,
                :,
            ]
            result = result + taps * kernel[3 * row_off + col_off]
    return result


def dilated_back(field_f, kernel, grad_out, dilation):
    height, breadth = (field_f.shape[1], field_f.shape[2])
    widths = ((0, 0), (dilation, dilation), (dilation, dilation), (0, 0))
    padded_field = jnp.pad(field_f, widths)
    padded_grad = jnp.pad(grad_out, widths)
    field_grad = jnp.zeros_like(field_f)
    kernel_rows = []
    for row_off in range(3):
        for col_off in range(3):
            taps = padded_field[
                :,
                row_off * dilation : row_off * dilation + height,
                col_off * dilation : col_off * dilation + breadth,
                :,
            ]
            kernel_rows.append(jnp.sum(taps * grad_out, axis=(0, 1, 2)))
            back_row = (2 - row_off) * dilation
            back_col = (2 - col_off) * dilation
            field_grad = (
                field_grad
                + padded_grad[:, back_row : back_row + height, back_col : back_col + breadth, :]
                * kernel[3 * row_off + col_off]
            )
    return (field_grad, jnp.stack(kernel_rows))


def shards(tiles, counts, cells, block_in, block_out, proj, depth, point, bias, cotangent):
    n_pipe = lax.axis_size("pipe")
    segment_id = lax.axis_index("pipe")
    micro_n, slot_n, pos_n, width_n = (
        tiles.shape[0],
        tiles.shape[2],
        tiles.shape[3],
        tiles.shape[4],
    )
    chan_q = proj.shape[1]
    cell_n = GH * GW
    slot_ids = jnp.arange(slot_n, dtype=jnp.int32)
    is_live = slot_ids[None, :] < counts
    placed = (
        (cells[:, 0, :, None] == jnp.arange(cell_n, dtype=jnp.int32)[None, None, :])
        & is_live[:, :, None]
    ).astype(jnp.bfloat16)
    occupied = jnp.sum(placed.astype(jnp.float32), axis=1)[:, :, None]
    encoder_in = tiles[:, 0]
    slot_m = encoder_in.shape[1]
    row_blocks = encoder_in.reshape(micro_n, slot_m * pos_n, width_n)
    w_in = block_in[0]
    w_out = block_out[0]
    carried = jnp.zeros_like(row_blocks[0])
    finished = []
    for tick_id in range(micro_n + n_pipe - 1):
        fresh = row_blocks[tick_id] if tick_id < micro_n else jnp.zeros_like(row_blocks[0])
        entering = jnp.where(segment_id == 0, fresh, carried)
        leaving = encode_block(entering, w_in, w_out)
        if tick_id >= n_pipe - 1:
            finished.append(leaving)
        if tick_id < micro_n + n_pipe - 2:
            carried = passed_along(leaving, "pipe", 1)
    stacked = jnp.stack(finished).reshape(micro_n, slot_m, pos_n, width_n)
    pooled_last = (jnp.sum(stacked.astype(jnp.float32), axis=2) / pos_n).astype(jnp.bfloat16)
    pooled = broadcast(pooled_last, "pipe", n_pipe - 1)
    features = jnp.einsum("mtc,cf->mtf", pooled, proj, preferred_element_type=jnp.float32).astype(
        jnp.bfloat16
    )
    cell_grid = jnp.einsum(
        "mjc,mjf->mcf", placed, features, preferred_element_type=jnp.float32
    ).astype(jnp.bfloat16)
    saved = []
    for layer_id in range(LAYERS):
        dilation = 2 ** (layer_id + 1)
        field_f = cell_grid.astype(jnp.float32).reshape(micro_n, GH, GW, chan_q)
        spread_u = (
            dilated(field_f, depth[layer_id], dilation)
            .reshape(micro_n, cell_n, chan_q)
            .astype(jnp.bfloat16)
        )
        partial_mix = jnp.einsum(
            "mcq,qf->mcf", spread_u, point[layer_id], preferred_element_type=jnp.float32
        )
        pre_act = (
            lax.psum_scatter(
                partial_mix.astype(jnp.bfloat16), "pipe", scatter_dimension=2, tiled=True
            ).astype(jnp.float32)
            + bias[layer_id][None, None, :]
        )
        saved.append((cell_grid, spread_u, pre_act))
        cell_grid = ((cell_grid.astype(jnp.float32) + jax.nn.gelu(pre_act)) * occupied).astype(
            jnp.bfloat16
        )
    mixed = cell_grid.reshape(micro_n, 1, cell_n, chan_q)
    upstream = cotangent[:, 0].astype(jnp.float32)
    point_grads = [None] * LAYERS
    depth_grads = [None] * LAYERS
    bias_grads = [None] * LAYERS
    for layer_id in reversed(range(LAYERS)):
        dilation = 2 ** (layer_id + 1)
        grid_in, spread_u, pre_act = saved[layer_id]
        masked = upstream * occupied
        slope_grad = jax.vjp(jax.nn.gelu, pre_act)[1](masked)[0]
        bias_grad = jnp.sum(slope_grad, axis=(0, 1))
        slope_half = slope_grad.astype(jnp.bfloat16)
        slope_all = lax.all_gather(slope_half, "pipe", axis=2, tiled=True)
        point_grad = jnp.einsum(
            "mcq,mcf->qf", spread_u, slope_all, preferred_element_type=jnp.float32
        )
        spread_grad = jnp.einsum(
            "mcf,qf->mcq", slope_all, point[layer_id], preferred_element_type=jnp.float32
        )
        field_grad, depth_grad = dilated_back(
            grid_in.astype(jnp.float32).reshape(micro_n, GH, GW, chan_q),
            depth[layer_id],
            spread_grad.reshape(micro_n, GH, GW, chan_q),
            dilation,
        )
        upstream = masked + field_grad.reshape(micro_n, cell_n, chan_q)
        point_grads[layer_id] = point_grad
        depth_grads[layer_id] = depth_grad
        bias_grads[layer_id] = bias_grad
    tile_grad = jnp.einsum(
        "mjc,mcf->mjf", placed.astype(jnp.float32), upstream, precision=lax.Precision.HIGHEST
    ).astype(jnp.bfloat16)
    proj_grad = jnp.einsum("mtc,mtf->cf", pooled, tile_grad, preferred_element_type=jnp.float32)
    proj_grad, point_all = (
        lax.psum_scatter(proj_grad, "dp", scatter_dimension=0, tiled=True),
        lax.psum_scatter(jnp.stack(point_grads), "dp", scatter_dimension=2, tiled=True),
    )
    depth_all, bias_all = lax.psum((jnp.stack(depth_grads), jnp.stack(bias_grads)), "dp")
    return (mixed, proj_grad, point_all, depth_all, bias_all)


def solution(mesh):
    in_specs = (
        P(None, "dp", None, None, None),
        P(None, "dp"),
        P(None, "dp", None),
        P("pipe", None, None),
        P("pipe", None, None),
        P(None, "pipe"),
        P(None, None, "pipe"),
        P(None, "pipe", None),
        P(None, "pipe"),
        P(None, "dp", None, "pipe"),
    )
    out_specs = (
        P(None, "dp", None, "pipe"),
        P("dp", "pipe"),
        P(None, "pipe", "dp"),
        P(None, None, "pipe"),
        P(None, "pipe"),
    )
    return jax.shard_map(shards, mesh=mesh, in_specs=in_specs, out_specs=out_specs, check_vma=False)
```

profile of v0, /device:TPU:1, one launch (start us, length us, event | category | flops | bytes accessed | tf_op | source)
XLA Modules:
  0.0 1283.9 jit_solution(17554314942541385586)
XLA Ops:
  7.2 4.3 fusion.3
  12.8 5.0 collective-permute-done
  17.8 4.5 maximum_convert_fusion.1
  23.5 2.8 collective-permute-done.1
  26.4 4.1 fusion.112
  33.4 30.5 %all-reduce.9.cloned.1.call-done = bf16[2,16,2048]{2,1,0:T(8,128)(2,1)} async-done(((bf16[2,16,2048]{2,1,0:T(8,128)(2,1)}), bf16[2,16,2048]{2,1,0:T(8,128)(2,1)}) %all-reduce.9.cloned.1.call-update) | async-done | bytes 131088 | tf_op jit(solution)/shard_map/psum | solution.py:19
  63.9 3.1 fusion.80
  67.0 6.8 add_convert_fusion.1
  74.8 4.2 convolution_convert_fusion.1
  79.2 15.6 %reduce-scatter.4.cloned.1.call-done = bf16[2,256,768]{2,1,0:T(8,128)(2,1)} async-done(((bf16[2,256,1536]{2,1,0:T(8,128)(2,1)}), bf16[2,256,768]{2,1,0:T(8,128)(2,1)}) %reduce-scatter.4.cloned.1.call-update) | async-done | bytes 786448 | tf_op jit(solution)/shard_map/reduce_scatter | solution.py:129
  99.3 4.2 convolution_convert_fusion
  103.5 15.8 %reduce-scatter.6.cloned.1.call-done = bf16[2,256,768]{2,1,0:T(8,128)(2,1)} async-done(((bf16[2,256,1536]{2,1,0:T(8,128)(2,1)}), bf16[2,256,768]{2,1,0:T(8,128)(2,1)}) %reduce-scatter.6.cloned.1.call-update) | async-done | bytes 786448 | tf_op jit(solution)/shard_map/reduce_scatter | solution.py:129
  119.4 4.0 fusion.154
  123.7 16.4 %all-gather.3.cloned.1.call-done = bf16[2,256,1536]{2,1,0:T(8,128)(2,1)} async-done(((bf16[2,256,768]{2,1,0:T(8,128)(2,1)}), bf16[2,256,1536]{2,1,0:T(8,128)(2,1)}) %all-gather.3.cloned.1.call-update) | async-done | bytes 1572880 | tf_op jit(solution)/shard_map/all_gather | solution.py:150
  140.1 4.9 multiply_reduce_fusion
  149.0 5.2 convolution_bitcast_fusion
  154.2 11.3 all-gather.5.cloned.1.call-done
  165.5 3.2 convolution_bitcast_fusion.1
  168.7 4.5 pad_maximum_fusion
  173.2 14.8 %copy.29 = f32[2,768,1536]{1,0,2:T(2,128)} copy(f32[2,768,1536]{2,1,0:T(8,128)} %pad_maximum_fusion) | data formatting | bytes 18874368 | tf_op jit(solution)/shard_map/stack | solution.py:173
  188.1 5.0 multiply_reduce_fusion.9
  196.3 3.8 convolution_bitcast_fusion.2
  202.8 581.5 %all-reduce.5 = (f32[2,9,768]{2,1,0:T(8,128)S(1)}, f32[2,768]{1,0:T(2,128)}) all-reduce(f32[2,9,768]{2,1,0:T(8,128)S(1)} %pad_maximum_fusion.1, f32[2,768]{1,0:T(2,128)S(1)} %pad_maximum_fusion.2), channel_id=1, replica_groups=mesh['pipe'=2,'dp'=128] {'dp'}, use_global_device_ids=true, to_apply=%region_25.26 | all-reduce | flops 15360 | bytes 122880 | tf_op jit(solution)/shard_map/psum | solution.py:175
  786.4 490.6 %reduce-scatter.8.cloned.1.call-done = f32[16,768]{1,0:T(8,128)} async-done(((f32[2048,768]{1,0:T(8,128)}), f32[16,768]{1,0:T(8,128)}) %reduce-scatter.8.cloned.1.call-update) | async-done | bytes 49168 | tf_op jit(solution)/shard_map/reduce_scatter | solution.py:172
  (87 shorter events, 22.1 us)
Async XLA Ops:
  7.2 56.8 %copy-start = (bf16[2048,768]{1,0:T(8,128)(2,1)S(1)}, bf16[2048,768]{1,0:T(8,128)(2,1)}, u32[]{:S(2)}) copy-start(bf16[2048,768]{1,0:T(8,128)(2,1)} %param.15) | copy-start | bytes 9437188
  7.2 56.7 %all-reduce.9.cloned.1.call-start = ((), (), s32[]{:S(2)}) async-start(), calls=%async_computation.3 | async-start | bytes 262144 | tf_op jit(solution)/shard_map/psum | solution.py:19
  11.5 6.3 collective-permute-start
  22.2 4.1 collective-permute-start.1
  30.5 2.7 copy-start.13
  30.5 2.8 copy-start.10
  30.5 33.4 %copy-start.11 = (s32[2,1,16]{2,1,0:T(1,128)S(1)}, s32[2,1,16]{2,1,0:T(1,128)}, u32[]{:S(2)}) copy-start(s32[2,1,16]{2,1,0:T(1,128)} %param.12) | copy-start | bytes 388
  33.2 61.6 %reduce-scatter.4.cloned.1.call-start = ((), (), s32[]{:S(2)}) async-start(), calls=%async_computation.4 | async-start | bytes 2359296 | tf_op jit(solution)/shard_map/reduce_scatter | solution.py:129
  73.9 0.9 copy-start.6
  74.7 4.3 copy-start.12
  79.0 15.8 %copy-start.3 = (f32[2,256,768]{2,1,0:T(8,128)S(1)}, f32[2,256,768]{2,1,0:T(8,128)}, u32[]{:S(2)}) copy-start(f32[2,256,768]{2,1,0:T(8,128)} %fusion.80) | copy-start | bytes 4718596
  79.0 40.4 %reduce-scatter.6.cloned.1.call-start = ((), (), s32[]{:S(2)}) async-start(), calls=%async_computation.5 | async-start | bytes 2359296 | tf_op jit(solution)/shard_map/reduce_scatter | solution.py:129
  98.4 0.9 copy-start.8
  103.5 36.6 %all-gather.3.cloned.1.call-start = ((), (), s32[]{:S(2)}) async-start(), calls=%async_computation.6 | async-start | bytes 2359296 | tf_op jit(solution)/shard_map/all_gather | solution.py:150
  123.4 42.1 %all-gather.5.cloned.1.call-start = ((), (), s32[]{:S(2)}) async-start(), calls=%async_computation.7 | async-start | bytes 2359296 | tf_op jit(solution)/shard_map/all_gather | solution.py:150
  145.1 1.3 copy-start.4
  145.1 1.4 copy-start.7
  148.9 636.0 %all-reduce.11.cloned.1.call-start = ((), (), s32[]{:S(2)}) async-start(), calls=%async_computation.9 | async-start | bytes 18874368
  165.5 3.2 copy-start.2
  188.1 1088.9 %reduce-scatter.8.cloned.1.call-start = ((), (), s32[]{:S(2)}) async-start(), calls=%async_computation.8 | async-start | bytes 6340608 | tf_op jit(solution)/shard_map/reduce_scatter | solution.py:172
  193.1 1.9 copy-start.5
  195.4 0.9 copy-start.9
  200.1 0.7 copy-start.14
  200.2 1076.8 %copy-start.1 = (bf16[2048,768]{1,0:T(8,128)(2,1)S(1)}, bf16[2048,768]{1,0:T(8,128)(2,1)}, u32[]{:S(2)}) copy-start(bf16[2048,768]{1,0:T(8,128)(2,1)} %param.15) | copy-start | bytes 9437188
Sparse Core Ops, SparseCore 0:
  33.3 30.5 all-reduce.8
  79.1 15.6 reduce-scatter.3
  103.6 15.7 reduce-scatter.5
  123.6 16.5 all-gather.2
  149.0 16.4 all-gather.4
  188.2 271.2 all-reduce.10
  466.6 810.3 reduce-scatter.7
where the time goes:
time: 1290 us; the launch traced here: 1280 us
  waiting for transfers between devices  588 us (46%)
  blocking collectives  581 us (45%)
  matrix products  47.2 us (4%)
  other arithmetic  27.7 us (2%)
  local copies, waits for them, and re-layouts  20.8 us (2%)
  between operations  15.5 us (1%)
    psum x1, blocking collectives, shards(): lax.psum((jnp.stack(depth_grads), jnp.stack(bias_grads)), 'dp')  581 us
    reduce_scatter x1, waiting for transfers between devices, shards(): lax.psum_scatter(proj_grad, 'dp', scatter_dimension=0, tiled=True)  491 us
    reduce_scatter x2, waiting for transfers between devices, shards(): lax.psum_scatter(partial_mix.astype(jnp.bfloat16), 'pipe', scatter_dimens...  31.4 us
    psum x1, waiting for transfers between devices, broadcast(): return lax.psum(block, axis)  30.5 us
    all_gather x2, waiting for transfers between devices, shards(): slope_all = lax.all_gather(slope_half, 'pipe', axis=2, tiled=True)  27.8 us
  transfers between devices with their start and end apart: 9, of which 8 were waited for; matrix products, arithmetic and copies ran while one was open for 2% of the time, Pallas kernels for 0%

commit v1 on v0

v1 whole, which is shorter than its diff:
```python
import jax
import jax.numpy as jnp
from jax import lax
from jax.experimental import pallas as pl
from jax.experimental.pallas import tpu as pltpu
from jax.sharding import Mesh, PartitionSpec as P

MB = 2
OWN = 16
POS = 8
ROWS = MB * OWN
CH = 2048
FEAT = 1536
HALF = 768
CELLS = 256
NZ, NY, NX = 8, 4, 4
PLANE = NY * NX
COLS = 12
BF = jnp.bfloat16
F32 = jnp.float32
VM = pl.BlockSpec(memory_space=pltpu.VMEM)
SM = pl.BlockSpec(memory_space=pltpu.SMEM)
PARAMS = pltpu.CompilerParams(vmem_limit_bytes=48 * 1024 * 1024)
TG, SP, SL, DG = 0, 32, 96, 112
MSG = 144


def dot(a, b):
    return jnp.dot(a, b, preferred_element_type=F32)


def iota(shape, axis):
    return lax.broadcasted_iota(jnp.int32, shape, axis)


def slot_maps(cells_ref, counts_ref):
    rows, cols = iota((ROWS, ROWS), 0), iota((ROWS, ROWS), 1)
    cell_r = jnp.zeros((ROWS, ROWS), jnp.int32)
    cell_c = jnp.zeros((ROWS, ROWS), jnp.int32)
    for m in range(MB):
        for j in range(OWN):
            cell = cells_ref[m, 0, j]
            cell_r = jnp.where(rows == m * OWN + j, cell, cell_r)
            cell_c = jnp.where(cols == m * OWN + j, cell, cell_c)
    live_r = (rows & (OWN - 1)) < jnp.where(rows < OWN, counts_ref[0, 0], counts_ref[1, 0])
    live_c = (cols & (OWN - 1)) < jnp.where(cols < OWN, counts_ref[0, 0], counts_ref[1, 0])
    pair = live_r & live_c & ((rows >> 4) == (cols >> 4))
    down = (cell_c >> 4) - (cell_r >> 4)
    right = (cell_c & 15) - (cell_r & 15)
    return pair, down, right


def tap_matrix(maps, dilation):
    pair, down, right = maps
    taps = []
    for a in range(3):
        for b in range(3):
            hit = pair & (down == (a - 1) * dilation) & (right == (b - 1) * dilation)
            taps.append(jnp.where(hit, 1.0, 0.0))
    return jnp.concatenate(taps, axis=0).astype(BF)


def live_rows(counts_ref, width):
    rows = iota((ROWS, width), 0)
    return (rows & (OWN - 1)) < jnp.where(rows < OWN, counts_ref[0, 0], counts_ref[1, 0])


def placed(cells_ref, counts_ref, m):
    rows, cols = iota((OWN, CELLS), 0), iota((OWN, CELLS), 1)
    cell = jnp.zeros((OWN, CELLS), jnp.int32)
    for j in range(OWN):
        cell = jnp.where(rows == j, cells_ref[m, 0, j], cell)
    return jnp.where((cell == cols) & (rows < counts_ref[m, 0]), 1.0, 0.0)


def weighted(shifted, depth_ref, layer, backward=False):
    total = None
    for t in range(9):
        s = 8 - t if backward else t
        term = shifted[s * ROWS : (s + 1) * ROWS] * depth_ref[layer, t : t + 1, :]
        total = term if total is None else total + term
    return total


def gelu_parts(x):
    c = 0.7978845608028654
    t = jnp.tanh(c * (x + 0.044715 * (x * x * x)))
    half = 0.5 * (1.0 + t)
    slope = half + 0.5 * x * (1.0 - t * t) * (c * (1.0 + 3 * 0.044715 * (x * x)))
    return x * half, slope


def whole(p_ref, own, other):
    first = p_ref[0] == 0
    return jnp.concatenate([jnp.where(first, own, other), jnp.where(first, other, own)], axis=1)


def encode(x_ref, w_in_ref, w_out_ref):
    x = x_ref[...]
    hidden = jnp.maximum(dot(x, w_in_ref[0]), 0.0).astype(BF)
    return jnp.maximum(x.astype(F32) + dot(hidden, w_out_ref[0]), 0.0).astype(BF)


def first_section(x_ref, w_in_ref, w_out_ref, out_ref):
    out_ref[...] = encode(x_ref, w_in_ref, w_out_ref)


def second_section(x_ref, w_in_ref, w_out_ref, out_ref):
    n = ROWS * POS
    pool = jnp.where(iota((ROWS, n), 1) >> 3 == iota((ROWS, n), 0), 1.0 / POS, 0.0).astype(BF)
    out_ref[...] = dot(pool, encode(x_ref, w_in_ref, w_out_ref)).astype(BF)


def enter(p_ref, cells_ref, counts_ref, mine_ref, got_ref, proj_ref, depth_ref, point_ref,
          bias_ref, cot_ref, pooled_ref, feat_ref, spread_ref, part_ref, msg_ref):
    pooled = jnp.where(p_ref[0] == 1, mine_ref[...], got_ref[...])
    pooled_ref[...] = pooled
    feat = jnp.where(live_rows(counts_ref, HALF), dot(pooled, proj_ref[...]), 0.0).astype(BF)
    feat_ref[...] = feat
    maps = slot_maps(cells_ref, counts_ref)
    spread = weighted(dot(tap_matrix(maps, 2), feat), depth_ref, 0).astype(BF)
    spread_ref[...] = spread
    left = dot(spread, point_ref[0, :, :HALF])
    right = dot(spread, point_ref[0, :, HALF:])
    first = p_ref[0] == 0
    part_ref[...] = jnp.where(first, left, right)
    msg_ref[:ROWS] = jnp.where(first, right, left)
    for m in range(MB):
        rows = dot(placed(cells_ref, counts_ref, m).astype(BF), cot_ref[m, 0])
        msg_ref[ROWS + m * OWN : ROWS + (m + 1) * OWN] = rows
    msg_ref[2 * ROWS :] = jnp.broadcast_to(bias_ref[1:2], (8, HALF))


def second_layer(cells_ref, counts_ref, part_ref, got_ref, feat_ref, bias_ref, depth_ref,
                 point_ref, pre_ref, grid_ref, spread_ref, mix_ref):
    pre = part_ref[...] + got_ref[:ROWS] + bias_ref[0:1]
    pre_ref[...] = pre
    value = feat_ref[...].astype(F32) + gelu_parts(pre)[0]
    grid = jnp.where(live_rows(counts_ref, HALF), value, 0.0).astype(BF)
    grid_ref[...] = grid
    maps = slot_maps(cells_ref, counts_ref)
    spread = weighted(dot(tap_matrix(maps, 4), grid), depth_ref, 1).astype(BF)
    spread_ref[...] = spread
    mix_ref[...] = dot(spread, point_ref[0])


def split_taps(taps, value):
    high = value.astype(BF)
    low = (value - high.astype(F32)).astype(BF)
    return dot(taps, high) + dot(taps, low)


def turn(p_ref, cells_ref, counts_ref, mix_ref, got_mix_ref, msg_ref, got_ref, pre_ref, grid_ref,
         depth_ref, point_ref, mixed_ref, slope1_ref, slope0_ref, masked_ref, grads_ref):
    cot = msg_ref[ROWS : 2 * ROWS]
    cot_all = whole(p_ref, cot, got_ref[ROWS : 2 * ROWS])
    bias_all = whole(p_ref, msg_ref[2 * ROWS :], got_ref[2 * ROWS :])[0:1]
    pre = mix_ref[...] + got_mix_ref[...] + bias_all
    value, deriv = gelu_parts(pre)
    slope = cot_all * deriv
    slope_half = slope.astype(BF)
    slope1_ref[...] = slope_half
    first = p_ref[0] == 0
    value = jnp.where(first, value[:, :HALF], value[:, HALF:])
    slope = jnp.where(first, slope[:, :HALF], slope[:, HALF:])
    grid = grid_ref[...]
    live = live_rows(counts_ref, HALF)
    mixed = jnp.where(live, grid.astype(F32) + value, 0.0).astype(BF)
    for m in range(MB):
        mixed_ref[m, 0] = lax.dot_general(
            placed(cells_ref, counts_ref, m).astype(BF), mixed[m * OWN : (m + 1) * OWN],
            (((0,), (0,)), ((), ())), preferred_element_type=F32).astype(BF)
    spread_grad = lax.dot_general(slope_half, point_ref[0], (((1,), (1,)), ((), ())),
                                  preferred_element_type=F32)
    taps = tap_matrix(slot_maps(cells_ref, counts_ref), 4)
    field = dot(taps, grid)
    rows = iota((16, HALF), 0)
    grads = jnp.where(rows == 9, jnp.sum(slope, axis=0, keepdims=True), 0.0)
    for t in range(9):
        row = jnp.sum(field[t * ROWS : (t + 1) * ROWS] * spread_grad, axis=0, keepdims=True)
        grads = jnp.where(rows == t, row, grads)
    back = weighted(split_taps(taps, spread_grad), depth_ref, 1, backward=True)
    masked = jnp.where(live, cot + back, 0.0)
    masked_ref[...] = masked
    slope0 = masked * gelu_parts(pre_ref[...])[1]
    slope0_ref[...] = slope0.astype(BF)
    grads_ref[...] = jnp.where(rows == 10, jnp.sum(slope0, axis=0, keepdims=True), grads)


def column_picker(depth, step, keep):
    rows, cols = iota((2 * depth, PLANE * 128), 0), iota((2 * depth, PLANE * 128), 1)
    row = iota((2 * depth, 1), 0)
    second = row >= depth
    rest = jnp.where(second, row - depth, row)
    group = jnp.zeros_like(rest)
    for g in range(1, PLANE):
        group = group + jnp.where(rest >= g * keep, 1, 0)
    target = group * 128 + (rest - group * keep) + jnp.where(second, step, 0)
    del rows
    return jnp.where(cols == target, 1.0, 0.0).astype(BF)


def picked(value, depth, keep):
    count = value.shape[0]
    parts = [value[:, 2 * depth * i : 2 * depth * (i + 1)] for i in range(4)]
    spread = dot(jnp.concatenate(parts, axis=0), column_picker(depth, 16, keep))
    out = []
    for g in range(PLANE):
        total = spread[:count, g * 128 : (g + 1) * 128]
        for i in range(1, 4):
            piece = spread[i * count : (i + 1) * count, g * 128 : (g + 1) * 128]
            total = total + pltpu.roll(piece, 32 * i, 1)
        out.append(total.astype(BF))
    return out


def leave(p_ref, cells_ref, counts_ref, slope0_ref, got_ref, slope1_ref, feat_ref, spread0_ref,
          spread1_ref, depth_ref, point_ref, masked_ref, grads_ref, pooled_ref, out_ref):
    slope0 = whole(p_ref, slope0_ref[...], got_ref[...])
    spread_grad = lax.dot_general(slope0, point_ref[0], (((1,), (1,)), ((), ())),
                                  preferred_element_type=F32)
    taps = tap_matrix(slot_maps(cells_ref, counts_ref), 2)
    field = dot(taps, feat_ref[...])
    rows = iota((32, HALF), 0)
    grads = jnp.concatenate([grads_ref[...], jnp.zeros((16, HALF), F32)], axis=0)
    for t in range(9):
        row = jnp.sum(field[t * ROWS : (t + 1) * ROWS] * spread_grad, axis=0, keepdims=True)
        grads = jnp.where(rows == (11 + t if t < 5 else 23 + t), row, grads)
    grads = grads.astype(BF)
    back = weighted(split_taps(taps, spread_grad), depth_ref, 0, backward=True)
    tile_grad = jnp.where(live_rows(counts_ref, HALF), masked_ref[...] + back, 0.0).astype(BF)
    slopes = picked(jnp.concatenate([slope0, slope1_ref[...]], axis=0), 192, COLS)
    pooled = picked(pooled_ref[...], 256, 16)
    for g in range(PLANE):
        out_ref[g, TG : TG + ROWS] = tile_grad
        out_ref[g, SP : SP + ROWS] = spread0_ref[...]
        out_ref[g, SP + ROWS : SP + 2 * ROWS] = spread1_ref[...]
        for side in range(2):
            r = slice(16 * side, 16 * side + 16)
            at = 384 * side
            out_ref[g, SL : SL + 16, at : at + 128] = slopes[g][r]
            out_ref[g, SL : SL + 16, at + 128 : at + 256] = slopes[g][32 + 16 * side : 48 + 16 * side]
            out_ref[g, SL : SL + 16, at + 256 : at + 384] = pooled[g][r]
        out_ref[g, DG : DG + 32] = grads


def products(in_ref, out_ref):
    n = PLANE * ROWS

    def rows_at(start):
        return in_ref[:, start : start + ROWS, :].reshape(n, HALF)

    def cols_at(lane):
        parts = [in_ref[:, SL : SL + 16, lane + 384 * s : lane + 384 * s + 128] for s in range(2)]
        return jnp.concatenate(parts, axis=1).reshape(n, 128)

    def outer(a, b):
        return lax.dot_general(a, b, (((0,), (0,)), ((), ())), preferred_element_type=F32)

    point0 = outer(cols_at(0), rows_at(SP))
    point1 = outer(cols_at(128), rows_at(SP + ROWS))
    proj = outer(cols_at(256), rows_at(TG))
    grads = in_ref[0, DG : DG + 32, :].astype(F32)
    for g in range(1, PLANE):
        grads = grads + in_ref[g, DG : DG + 32, :].astype(F32)
    for z in range(NZ):
        r = slice(16 * z, 16 * z + 16)
        out_ref[z, 0:16] = (point0[r] + grads[16:32]).astype(BF)
        out_ref[z, 16:32] = point1[r].astype(BF)
        out_ref[z, 32:48] = proj[r].astype(BF)
        out_ref[z, 48:64] = grads[0:16].astype(BF)


def finish(in_ref, proj_ref, point_ref, depth_ref, bias_ref):
    total = in_ref[0].astype(F32)
    for z in range(1, NZ):
        total = total + in_ref[z].astype(F32)
    proj_ref[...] = total[32:48]
    for layer in range(2):
        point_ref[layer] = total[16 * layer : 16 * layer + 16].T[:, :COLS]
    depth_ref[1] = total[48:57]
    bias_ref[1:2] = total[57:58]
    bias_ref[0:1] = total[58:59]
    depth_ref[0, 0:5] = total[59:64]
    depth_ref[0, 5:9] = total[12:16]


def call(body, outs, specs, *args):
    return pl.pallas_call(
        body, out_shape=[jax.ShapeDtypeStruct(s, d) for s, d in outs], in_specs=specs, grid=(1,),
        out_specs=[VM] * len(outs), compiler_params=PARAMS, name=body.__name__)(*args)


def layer_of(i):
    return pl.BlockSpec((1, HALF, FEAT), lambda _: (i, 0, 0))


def swap(value):
    return lax.ppermute(value, "pipe", [(0, 1), (1, 0)])


def shards(tiles, counts, cells, block_in, block_out, proj, depth, point, bias, cotangent):
    p = lax.axis_index("pipe").astype(jnp.int32).reshape(1)
    x = tiles.reshape(ROWS * POS, CH)
    (x,) = call(first_section, [(x.shape, BF)], [VM] * 3, x, block_in, block_out)
    x = lax.ppermute(x, "pipe", [(0, 1)])
    (mine,) = call(second_section, [((ROWS, CH), BF)], [VM] * 3, x, block_in, block_out)
    got = lax.ppermute(mine, "pipe", [(1, 0)])
    half_b, half_f = ((ROWS, HALF), BF), ((ROWS, HALF), F32)
    pooled, feat, spread0, part, msg = call(
        enter, [((ROWS, CH), BF), half_b, half_b, half_f, ((2 * ROWS + 8, HALF), F32)],
        [SM, SM, SM, VM, VM, VM, VM, layer_of(0), VM, VM],
        p, cells, counts, mine, got, proj, depth, point, bias, cotangent)
    got_msg = swap(msg)
    pre0, grid1, spread1, mix = call(
        second_layer, [half_f, half_b, half_b, ((ROWS, FEAT), F32)],
        [SM, SM, VM, VM, VM, VM, VM, layer_of(1)],
        cells, counts, part, got_msg, feat, bias, depth, point)
    got_mix = swap(mix)
    mixed, slope1, slope0, masked, grads = call(
        turn, [((MB, 1, CELLS, HALF), BF), ((ROWS, FEAT), BF), half_b, half_f, ((16, HALF), F32)],
        [SM, SM, SM] + [VM] * 7 + [layer_of(1)],
        p, cells, counts, mix, got_mix, msg, got_msg, pre0, grid1, depth, point)
    got_slope = swap(slope0)
    (rows,) = call(
        leave, [((PLANE, MSG, HALF), BF)],
        [SM, SM, SM] + [VM] * 7 + [layer_of(0)] + [VM] * 3,
        p, cells, counts, slope0, got_slope, slope1, feat, spread0, spread1, depth, point, masked,
        grads, pooled)
    rows = lax.all_to_all(rows, ("y", "x"), 0, 0, tiled=True)
    (sums,) = call(products, [((NZ, 64, HALF), BF)], [VM], rows)
    sums = lax.all_to_all(sums, "z", 0, 0, tiled=True)
    grad_proj, grad_point, grad_depth, grad_bias = call(
        finish, [((16, HALF), F32), ((2, HALF, COLS), F32), ((2, 9, HALF), F32), ((2, HALF), F32)],
        [VM], sums)
    return mixed, grad_proj, grad_point, grad_depth, grad_bias


def solution(mesh):
    grid = Mesh(mesh.devices.reshape(2, NZ, NY, NX), ("pipe", "z", "y", "x"))
    dp = ("z", "y", "x")
    in_specs = (
        P(None, dp, None, None, None),
        P(None, dp),
        P(None, dp, None),
        P("pipe", None, None),
        P("pipe", None, None),
        P(None, "pipe"),
        P(None, None, "pipe"),
        P(None, "pipe", None),
        P(None, "pipe"),
        P(None, dp, None, "pipe"),
    )
    out_specs = (
        P(None, dp, None, "pipe"),
        P(dp, "pipe"),
        P(None, "pipe", dp),
        P(None, None, "pipe"),
        P(None, "pipe"),
    )
    return jax.shard_map(shards, mesh=grid, in_specs=in_specs, out_specs=out_specs, check_vma=False)
```

time: 1290 us -> 117 us (0.09)
  waiting for transfers between devices: 588 us -> 9.27 us
  blocking collectives: 581 us -> 76.8 us
  matrix products: 47.2 us -> 0 us
  other arithmetic: 27.7 us -> 0.01 us
  Pallas kernels: 0 us -> 17.5 us
  between operations: 15.5 us -> 0.76 us
  local copies, waits for them, and re-layouts: 20.8 us -> 6.4 us
    psum x1 -> x0, blocking collectives: 581 us -> none  [shards(): lax.psum((jnp.stack(depth_grads), jnp.stack(bias_grads)), 'dp')]
    reduce_scatter x3 -> x0, waiting for transfers between devices: 522 us -> none  [the longest x1 491 us: shards(): lax.psum_scatter(proj_grad, 'dp', scatter_dimension=0, tiled=True)]
    all_to_all x0 -> x2, blocking collectives: none -> 76.8 us  [the longest x1 48.5 us: shards(): rows = lax.all_to_all(rows, ('y', 'x'), 0, 0, tiled=True)]
    dot_general x12 -> x0, matrix products: 47.2 us -> none  [the longest x3 12.9 us: encode_block(): jnp.dot(hidden, w_out, preferred_element_type=jnp.float32)]
    psum x1 -> x0, waiting for transfers between devices: 30.5 us -> none  [broadcast(): return lax.psum(block, axis)]
    all_gather x2 -> x0, waiting for transfers between devices: 27.8 us -> none  [shards(): slope_all = lax.all_gather(slope_half, 'pipe', axis=2, tiled=True)]
    pallas_call x0 -> x8, Pallas kernels: none -> 17.5 us  [call(): pl.pallas_call(body, out_shape=[jax.ShapeDtypeStruct(s, d) for s, d in ou...]
    another operation x23 -> x0, local copies, waits for them, and re-layouts: 15 us -> none  [the longest x1 14.8 us: shards(): jnp.stack(point_grads)]
  transfers between devices with their start and end apart: 9 -> 5, of which waited for: 8 -> 5; matrix products, arithmetic and copies ran while one was open for 2% -> 0% of each run, Pallas kernels for 0% -> 0%
where the time goes in v1:
time: 117 us; the launch traced here: 115 us
  blocking collectives  76.8 us (66%)
  Pallas kernels  17.5 us (15%)
  waiting for transfers between devices  9.27 us (8%)
  local copies, waits for them, and re-layouts  6.4 us (5%)
  starting transfers between devices  4.63 us (4%)
    all_to_all x1, blocking collectives, shards(): rows = lax.all_to_all(rows, ('y', 'x'), 0, 0, tiled=True)  48.5 us
    all_to_all x1, blocking collectives, shards(): sums = lax.all_to_all(sums, 'z', 0, 0, tiled=True)  28.3 us
    pallas_call x8, Pallas kernels, call(): pl.pallas_call(body, out_shape=[jax.ShapeDtypeStruct(s, d) for s, d in ou...  17.5 us
    unnamed x28, local copies, waits for them, and re-layouts  6.4 us
    ppermute x1, waiting for transfers between devices, shards(): x = lax.ppermute(x, 'pipe', [(0, 1)])  5.37 us
    ppermute x3, waiting for transfers between devices, swap(): return lax.ppermute(value, 'pipe', [(0, 1), (1, 0)])  3.07 us
  transfers between devices with their start and end apart: 5, of which 5 were waited for; matrix products, arithmetic and copies ran while one was open for 0% of the time, Pallas kernels for 0%

profile of v1, /device:TPU:1, one launch (start us, length us, event | category | flops | bytes accessed | tf_op | source)
XLA Modules:
  0.0 115.4 jit_solution(6207536357342919263)
XLA Ops:
  0.6 1.6 %copy-done = bf16[1,2048,512]{2,1,0:T(8,128)(2,1)S(1)} copy-done((bf16[1,2048,512]{2,1,0:T(8,128)(2,1)S(1)}, bf16[1,2048,512]{2,1,0:T(8,128)(2,1)}, u32[]{:S(2)}) %copy-start) | copy-done | bytes 2097176
  2.2 1.2 %copy-done.4 = bf16[2,1,16,8,2048]{4,3,2,1,0:T(8,128)(2,1)S(1)} copy-done((bf16[2,1,16,8,2048]{4,3,2,1,0:T(8,128)(2,1)S(1)}, bf16[2,1,16,8,2048]{4,3,2,1,0:T(8,128)(2,1)}, u32[]{:S(2)}) %copy-start.4) | copy-done | bytes 1048600
  3.5 3.1 %first_section.1 = bf16[256,2048]{1,0:T(8,128)(2,1)S(1)} custom-call(bf16[256,2048]{1,0:T(8,128)(2,1)S(1)} %bitcast.4, bf16[1,2048,512]{2,1,0:T(8,128)(2,1)S(1)} %copy-done, bf16[1,512,2048]{2,1,0:T(8,128)(2,1)} %w_out_ref.3), custom_call_target="tpu_custom_call" | custom-call | tf_op jit(solution)/shard_map/first_section/pallas_call | solution.py:289
  6.6 1.4 %collective-permute-start = (bf16[256,2048]{1,0:T(8,128)(2,1)S(1)}, bf16[256,2048]{1,0:T(8,128)(2,1)S(1)}, u32[]{:S(2)}, u32[]{:S(2)}) collective-permute-start(bf16[256,2048]{1,0:T(8,128)(2,1)S(1)} %first_section.1), channel_id=1, source_target_pairs={{0,128},{1,129},{2,130},{3,131},{4,132},{5,133},{6,134},{7,135},{8... | collective-permute-start | bytes 3145736 | tf_op jit(solution)/shard_map/ppermute | solution.py:306
  8.0 5.4 %collective-permute-done.x_ref = bf16[256,2048]{1,0:T(8,128)(2,1)S(1)} collective-permute-done((bf16[256,2048]{1,0:T(8,128)(2,1)S(1)}, bf16[256,2048]{1,0:T(8,128)(2,1)S(1)}, u32[]{:S(2)}, u32[]{:S(2)}) %collective-permute-start) | collective-permute-done | bytes 1048608 | tf_op jit(solution)/shard_map/ppermute | solution.py:306
  13.4 1.5 %second_section.1.mine_ref = bf16[32,2048]{1,0:T(8,128)(2,1)S(1)} custom-call(bf16[256,2048]{1,0:T(8,128)(2,1)S(1)} %collective-permute-done.x_ref, bf16[1,2048,512]{2,1,0:T(8,128)(2,1)S(1)} %copy-done.1, bf16[1,512,2048]{2,1,0:T(8,128)(2,1)S(1)} %copy-done.2), custom_call_target="tpu_custom_call" | custom-call | tf_op jit(solution)/shard_map/second_section/pallas_call | solution.py:289
  14.9 2.1 %collective-permute-start.1 = (bf16[32,2048]{1,0:T(8,128)(2,1)S(1)}, bf16[32,2048]{1,0:T(8,128)(2,1)S(1)}, u32[]{:S(2)}, u32[]{:S(2)}) collective-permute-start(bf16[32,2048]{1,0:T(8,128)(2,1)S(1)} %second_section.1.mine_ref), channel_id=1, source_target_pairs={{128,0},{129,1},{130,2},{131,3},{132,4},{133,5},{134,6},{135,7},{1... | collective-permute-start | bytes 393224 | tf_op jit(solution)/shard_map/ppermute | solution.py:308
  17.1 0.8 collective-permute-done.1.got_ref
  17.9 1.9 %copy-done.3 = bf16[2048,768]{1,0:T(8,128)(2,1)S(1)} copy-done((bf16[2048,768]{1,0:T(8,128)(2,1)S(1)}, bf16[2048,768]{1,0:T(8,128)(2,1)}, u32[]{:S(2)}) %copy-start.3) | copy-done | bytes 3145752
  19.8 3.3 %enter.1 = (bf16[32,2048]{1,0:T(8,128)(2,1)S(1)}, bf16[32,768]{1,0:T(8,128)(2,1)S(1)}, bf16[32,768]{1,0:T(8,128)(2,1)S(1)}, f32[32,768]{1,0:T(8,128)S(1)}, f32[72,768]{1,0:T(8,128)S(1)}) custom-call(s32[1]{0:T(128)} %bitcast.p_ref, s32[2,1,16]{2,1,0:T(1,128)S(1)} %copy-done.7, s32[2,1]{1,0:T(2,128)S(1)} %copy.19.counts_ref, ...), custom_call_target="tpu_custom_call" | custom-call | tf_op jit(solution)/shard_map/enter/pallas_call | solution.py:289
  23.1 0.4 collective-permute-start.2
  23.5 1.1 collective-permute-done.2.got_ref
  24.6 1.3 %second_layer.1 = (f32[32,768]{1,0:T(8,128)S(1)}, bf16[32,768]{1,0:T(8,128)(2,1)S(1)}, bf16[32,768]{1,0:T(8,128)(2,1)S(1)}, f32[32,1536]{1,0:T(8,128)S(1)}) custom-call(s32[2,1,16]{2,1,0:T(1,128)S(1)} %copy-done.7, s32[2,1]{1,0:T(2,128)S(1)} %copy.19.counts_ref, f32[32,768]{1,0:T(8,128)S(1)} %get-tuple-element.23.part_ref, ...), custom_call_target="tpu_custom_call" | custom-call | tf_op jit(solution)/shard_map/second_layer/pallas_call | solution.py:289
  25.9 0.4 collective-permute-start.3
  26.3 1.1 collective-permute-done.3.got_mix_ref
  27.4 2.9 %turn.1 = (bf16[2,1,256,768]{3,2,1,0:T(8,128)(2,1)}, bf16[32,1536]{1,0:T(8,128)(2,1)S(1)}, bf16[32,768]{1,0:T(8,128)(2,1)S(1)}, f32[32,768]{1,0:T(8,128)S(1)}, f32[16,768]{1,0:T(8,128)S(1)}) custom-call(s32[1]{0:T(128)} %bitcast.p_ref, s32[2,1,16]{2,1,0:T(1,128)S(1)} %copy-done.7, s32[2,1]{1,0:T(2,128)S(1)} %copy.19.counts_ref, ...), custom_call_target="tpu_custom_call" | custom-call | tf_op jit(solution)/shard_map/turn/pallas_call | solution.py:289
  30.7 0.9 collective-permute-done.4.got_ref
  31.6 4.0 %leave.1 = bf16[16,144,768]{2,1,0:T(8,128)(2,1)S(1)} custom-call(s32[1]{0:T(128)} %bitcast.p_ref, s32[2,1,16]{2,1,0:T(1,128)S(1)} %copy-done.7, s32[2,1]{1,0:T(2,128)S(1)} %copy.19.counts_ref, bf16[32,768]{1,0:T(8,128)(2,1)S(1)} %get-tuple-element.30.slope0_ref, bf16[32,768]{1,0:T(8,128)(2,1)S(1)} %collective-permute-done.4.got_ref, ...), custom_call_target="tpu_custom_call" | custom-call | tf_op jit(solution)/shard_map/leave/pallas_call | solution.py:289
  35.6 48.5 %all_to_all.10.in_ref = bf16[16,144,768]{2,1,0:T(8,128)(2,1)S(1)} all-to-all(bf16[16,144,768]{2,1,0:T(8,128)(2,1)S(1)} %leave.1), channel_id=1, replica_groups=mesh['pipe'=2,'z'=8,'y'=4,'x'=4] {'y','x'}, dimensions={0} | all-to-all | bytes 7077888 | tf_op jit(solution)/shard_map/all_to_all | solution.py:330
  84.1 0.5 products.1
  84.6 28.3 %all_to_all.11.in_ref = bf16[8,64,768]{2,1,0:T(8,128)(2,1)S(1)} all-to-all(bf16[8,64,768]{2,1,0:T(8,128)(2,1)S(1)} %products.1), channel_id=1, replica_groups=mesh['pipe'=2,'z'=8,'y'=4,'x'=4] {'z'}, dimensions={0} | all-to-all | bytes 1572864 | tf_op jit(solution)/shard_map/all_to_all | solution.py:332
  113.0 0.9 finish.1
  113.8 0.7 copy.24
  114.5 0.9 copy.23
  (25 shorter events, 0.5 us)
Async XLA Ops:
  0.6 1.6 %copy-start = (bf16[1,2048,512]{2,1,0:T(8,128)(2,1)S(1)}, bf16[1,2048,512]{2,1,0:T(8,128)(2,1)}, u32[]{:S(2)}) copy-start(bf16[1,2048,512]{2,1,0:T(8,128)(2,1)} %w_in_ref.3) | copy-start | bytes 6291460
  2.2 1.2 %copy-start.4 = (bf16[2,1,16,8,2048]{4,3,2,1,0:T(8,128)(2,1)S(1)}, bf16[2,1,16,8,2048]{4,3,2,1,0:T(8,128)(2,1)}, u32[]{:S(2)}) copy-start(bf16[2,1,16,8,2048]{4,3,2,1,0:T(8,128)(2,1)} %param.10) | copy-start | bytes 3145732
  3.4 10.0 %copy-start.1 = (bf16[1,2048,512]{2,1,0:T(8,128)(2,1)S(1)}, bf16[1,2048,512]{2,1,0:T(8,128)(2,1)}, u32[]{:S(2)}) copy-start(bf16[1,2048,512]{2,1,0:T(8,128)(2,1)} %w_in_ref.3) | copy-start | bytes 6291460
  3.5 10.0 %copy-start.2 = (bf16[1,512,2048]{2,1,0:T(8,128)(2,1)S(1)}, bf16[1,512,2048]{2,1,0:T(8,128)(2,1)}, u32[]{:S(2)}) copy-start(bf16[1,512,2048]{2,1,0:T(8,128)(2,1)} %w_out_ref.3) | copy-start | bytes 6291460
  6.5 10.4 %copy-start.9 = (s32[2,1]{0,1:T(1,128)S(1)}, s32[2,1]{0,1:T(1,128)}, u32[]{:S(2)}) copy-start(s32[2,1]{0,1:T(1,128)} %param.11) | copy-start | bytes 28
  6.6 10.5 %copy-start.8 = (f32[2,9,768]{2,0,1:T(2,128)S(1)}, f32[2,9,768]{2,0,1:T(2,128)}, u32[]{:S(2)}) copy-start(f32[2,9,768]{2,0,1:T(2,128)} %param.16) | copy-start | bytes 165892
  6.6 11.3 %copy-start.5 = (bf16[2,1,256,768]{3,2,1,0:T(8,128)(2,1)S(1)}, bf16[2,1,256,768]{3,2,1,0:T(8,128)(2,1)}, u32[]{:S(2)}) copy-start(bf16[2,1,256,768]{3,2,1,0:T(8,128)(2,1)} %cot_ref.1) | copy-start | bytes 2359300
  6.6 11.3 %copy-start.6 = (f32[2,768]{1,0:T(2,128)S(1)}, f32[2,768]{1,0:T(2,128)}, u32[]{:S(2)}) copy-start(f32[2,768]{1,0:T(2,128)} %bias_ref.3) | copy-start | bytes 18436
  6.6 11.3 %copy-start.7 = (s32[2,1,16]{2,1,0:T(1,128)S(1)}, s32[2,1,16]{2,1,0:T(1,128)}, u32[]{:S(2)}) copy-start(s32[2,1,16]{2,1,0:T(1,128)} %cells_ref.7) | copy-start | bytes 388
  6.6 6.8 %collective-permute-start = (bf16[256,2048]{1,0:T(8,128)(2,1)S(1)}, bf16[256,2048]{1,0:T(8,128)(2,1)S(1)}, u32[]{:S(2)}, u32[]{:S(2)}) collective-permute-start(bf16[256,2048]{1,0:T(8,128)(2,1)S(1)} %first_section.1), channel_id=1, source_target_pairs={{0,128},{1,129},{2,130},{3,131},{4,132},{5,133},{6,134},{7,135},{8... | collective-permute-start | bytes 3145736 | tf_op jit(solution)/shard_map/ppermute | solution.py:306
  13.4 11.2 %slice-start = ((s8[4718592]{0:T(1024)(128)(4,1)}), s8[524288]{0:T(1024)(128)(4,1)S(1)}, s32[]{:S(2)}) async-start(s8[4718592]{0:T(1024)(128)(4,1)} %bitcast.2), calls=%async_computation.2 | async-start | bytes 1048576
  14.9 3.0 %collective-permute-start.1 = (bf16[32,2048]{1,0:T(8,128)(2,1)S(1)}, bf16[32,2048]{1,0:T(8,128)(2,1)S(1)}, u32[]{:S(2)}, u32[]{:S(2)}) collective-permute-start(bf16[32,2048]{1,0:T(8,128)(2,1)S(1)} %second_section.1.mine_ref), channel_id=1, source_target_pairs={{128,0},{129,1},{130,2},{131,3},{132,4},{133,5},{134,6},{135,7},{1... | collective-permute-start | bytes 393224 | tf_op jit(solution)/shard_map/ppermute | solution.py:308
  17.9 1.9 %copy-start.3 = (bf16[2048,768]{1,0:T(8,128)(2,1)S(1)}, bf16[2048,768]{1,0:T(8,128)(2,1)}, u32[]{:S(2)}) copy-start(bf16[2048,768]{1,0:T(8,128)(2,1)} %proj_ref.1) | copy-start | bytes 9437188
  19.8 4.8 %slice-start.1 = ((s8[4718592]{0:T(1024)(128)(4,1)}), s8[4194304]{0:T(1024)(128)(4,1)S(1)}, s32[]{:S(2)}) async-start(s8[4718592]{0:T(1024)(128)(4,1)} %bitcast.2), calls=%async_computation.3 | async-start | bytes 8388608
  23.1 1.5 %collective-permute-start.2 = (f32[72,768]{1,0:T(8,128)S(1)}, f32[72,768]{1,0:T(8,128)S(1)}, u32[]{:S(2)}, u32[]{:S(2)}) collective-permute-start(f32[72,768]{1,0:T(8,128)S(1)} %get-tuple-element.24.msg_ref), channel_id=1, source_target_pairs={{0,128},{128,0},{1,129},{129,1},{2,130},{130,2},{3,131},{131,3},{4... | collective-permute-start | bytes 663560 | tf_op jit(solution)/shard_map/ppermute | solution.py:299
  25.9 1.5 %collective-permute-start.3 = (f32[32,1536]{1,0:T(8,128)S(1)}, f32[32,1536]{1,0:T(8,128)S(1)}, u32[]{:S(2)}, u32[]{:S(2)}) collective-permute-start(f32[32,1536]{1,0:T(8,128)S(1)} %get-tuple-element.26.mix_ref), channel_id=1, source_target_pairs={{0,128},{128,0},{1,129},{129,1},{2,130},{130,2},{3,131},{131,3},{4... | collective-permute-start | bytes 589832 | tf_op jit(solution)/shard_map/ppermute | solution.py:299
  30.3 1.2 %collective-permute-start.4 = (bf16[32,768]{1,0:T(8,128)(2,1)S(1)}, bf16[32,768]{1,0:T(8,128)(2,1)S(1)}, u32[]{:S(2)}, u32[]{:S(2)}) collective-permute-start(bf16[32,768]{1,0:T(8,128)(2,1)S(1)} %get-tuple-element.30.slope0_ref), channel_id=1, source_target_pairs={{0,128},{128,0},{1,129},{129,1},{2,130},{130,2},{3,131},{131,3},{4... | collective-permute-start | bytes 147464 | tf_op jit(solution)/shard_map/ppermute | solution.py:299

commit v2 on v0

v2 whole, which is shorter than its diff:
```python
import jax
import jax.numpy as jnp
from jax import lax
from jax.experimental import pallas as pl
from jax.experimental.pallas import tpu as pltpu
from jax.sharding import Mesh, PartitionSpec as P

MB = 2
OWN = 16
POS = 8
ROWS = MB * OWN
CH = 2048
FEAT = 1536
HALF = 768
CELLS = 256
NZ, NY, NX = 8, 4, 4
PLANE = NY * NX
ALL = NZ * ROWS
SLICE = CH // NZ
COLS = 12
WIDTH = HALF + SLICE
SIDE = HALF + 128
STEP = 16
BF = jnp.bfloat16
F32 = jnp.float32
VM = pl.BlockSpec(memory_space=pltpu.VMEM)
HB = pl.BlockSpec(memory_space=pltpu.HBM)
SM = pl.BlockSpec(memory_space=pltpu.SMEM)


def dot(a, b):
    return jnp.dot(a, b, preferred_element_type=F32)


def dot_nt(a, b):
    return lax.dot_general(a, b, (((1,), (1,)), ((), ())), preferred_element_type=F32)


def dot_tn(a, b):
    return lax.dot_general(a, b, (((0,), (0,)), ((), ())), preferred_element_type=F32)


def iota(shape, axis):
    return lax.broadcasted_iota(jnp.int32, shape, axis)


def halves():
    p = lax.axis_index("pipe")
    mine = pl.multiple_of(p * HALF, 128)
    other = pl.multiple_of((1 - p) * HALF, 128)
    return pl.ds(mine, HALF), pl.ds(other, HALF)


def own_live(counts_ref, width):
    rows = iota((ROWS, width), 0)
    return (rows & (OWN - 1)) < jnp.where(rows < OWN, counts_ref[0, 0], counts_ref[1, 0])


def wide(code, times):
    return jnp.concatenate([code.astype(F32)] * times, axis=1)


def live_at(side_ref, rows):
    return wide(side_ref[rows, HALF:], HALF // 128) >= 0


def taps(side_ref, near_ref, near_long_ref, far_ref, far_long_ref):
    code = wide(side_ref[:, HALF:], 2)
    rows, cols = code.astype(jnp.int32), code.T.astype(jnp.int32)
    block = (iota((ALL, ALL), 0) >> 4) == (iota((ALL, ALL), 1) >> 4)
    pair = block & (rows >= 0) & (cols >= 0)
    down = jnp.where(pair, (cols >> 4) - (rows >> 4), 64)
    right = (cols & 15) - (rows & 15)
    for dilation, out_ref, long_ref in ((2, near_ref, near_long_ref), (4, far_ref, far_long_ref)):
        for t in range(9):
            hit = (down == (t // 3 - 1) * dilation) & (right == (t % 3 - 1) * dilation)
            hit = jnp.where(hit, 1.0, 0.0).astype(BF)
            out_ref[:, t * ALL : (t + 1) * ALL] = hit
            long_ref[t * ALL : (t + 1) * ALL] = hit


def chunks():
    return [slice(i, i + STEP) for i in range(0, ALL, STEP)]


def put_weighed(stack, rows, value, depth_ref, layer, backward):
    for t in range(9):
        s = 8 - t if backward else t
        at = slice(t * ALL + rows.start, t * ALL + rows.stop)
        stack[at] = (value * depth_ref[s, layer : layer + 1, :]).astype(BF)


def depth_rows(long_ref, grid, grad, moved, out_ref, rows):
    moved[...] = dot(long_ref[...], grid)
    for at in (slice(0, 384), slice(384, HALF)):
        sums = [None] * 9
        for i in range(0, ALL, 8):
            value = grad[i : i + 8, at]
            for t in range(9):
                term = moved[t * ALL + i : t * ALL + i + 8, at] * value
                sums[t] = term if sums[t] is None else sums[t] + term
        for t in range(9):
            out_ref[rows[t] : rows[t] + 1, at] = jnp.sum(sums[t], axis=0, keepdims=True)


def gelu_parts(x):
    c = 0.7978845608028654
    t = jnp.tanh(c * (x + 0.044715 * (x * x * x)))
    half = 0.5 * (1.0 + t)
    slope = half + 0.5 * x * (1.0 - t * t) * (c * (1.0 + 3 * 0.044715 * (x * x)))
    return x * half, slope


def encode(x_ref, w_in_ref, w_out_ref):
    x = x_ref[...]
    hidden = jnp.maximum(dot(x, w_in_ref[0]), 0.0).astype(BF)
    return jnp.maximum(x.astype(F32) + dot(hidden, w_out_ref[0]), 0.0).astype(BF)


def first_section(x_hbm, w_in_hbm, w_out_hbm, out_ref, x_ref, w_in_ref, w_out_ref, sems):
    n = 4
    step = CH // n
    copies = []
    for k in range(n):
        at = pl.ds(k * step, step)
        copies.append(pltpu.make_async_copy(x_hbm.at[:, at], x_ref.at[:, at], sems.at[0, k]))
        copies.append(pltpu.make_async_copy(w_in_hbm.at[0, at], w_in_ref.at[at], sems.at[1, k]))
    for k in range(n):
        at = pl.ds(k * step, step)
        copies.append(pltpu.make_async_copy(w_out_hbm.at[0, :, at], w_out_ref.at[:, at], sems.at[2, k]))
    for copy in copies:
        copy.start()
    hidden = None
    for k in range(n):
        at = slice(k * step, (k + 1) * step)
        copies[2 * k].wait()
        copies[2 * k + 1].wait()
        part = dot(x_ref[:, at], w_in_ref[at])
        hidden = part if hidden is None else hidden + part
    hidden = jnp.maximum(hidden, 0.0).astype(BF)
    for k in range(n):
        at = slice(k * step, (k + 1) * step)
        copies[2 * n + k].wait()
        total = x_ref[:, at].astype(F32) + dot(hidden, w_out_ref[:, at])
        out_ref[:, at] = jnp.maximum(total, 0.0).astype(BF)


def second_section(x_ref, w_in_hbm, w_out_hbm, out_ref, w_in_ref, w_out_ref, sems):
    n = ROWS * POS
    ins, outs = [], []
    for k in range(2):
        at = pl.ds(k * (CH // 2), CH // 2)
        ins.append(pltpu.make_async_copy(w_in_hbm.at[0, at], w_in_ref.at[at], sems.at[0, k]))
        outs.append(
            pltpu.make_async_copy(w_out_hbm.at[0, :, at], w_out_ref.at[:, at], sems.at[1, k]))
    for copy in ins + outs:
        copy.start()
    pool = jnp.where(iota((ROWS, n), 1) >> 3 == iota((ROWS, n), 0), 1.0 / POS, 0.0).astype(BF)
    hidden = None
    for k in range(2):
        at = slice(k * (CH // 2), (k + 1) * (CH // 2))
        ins[k].wait()
        part = dot(x_ref[:, at], w_in_ref[at])
        hidden = part if hidden is None else hidden + part
    hidden = jnp.maximum(hidden, 0.0).astype(BF)
    for k in range(2):
        at = slice(k * (CH // 2), (k + 1) * (CH // 2))
        outs[k].wait()
        total = x_ref[:, at].astype(F32) + dot(hidden, w_out_ref[:, at])
        out_ref[:, at] = dot(pool, jnp.maximum(total, 0.0).astype(BF)).astype(BF)


def side_rows(cells_ref, counts_ref, cot_ref, out_ref):
    rows = iota((ROWS, 128), 0)
    code = jnp.zeros((ROWS, 128), jnp.int32)
    for m in range(MB):
        for j in range(OWN):
            code = jnp.where(rows == m * OWN + j, cells_ref[m, 0, j], code)
    code = jnp.where(own_live(counts_ref, 128), code, -1)
    double = jnp.concatenate([code, code], axis=1)
    code = code.astype(F32).astype(BF)
    hit = jnp.where(double == iota((ROWS, CELLS), 1), 1.0, 0.0).astype(BF)
    for m in range(MB):
        at = slice(m * OWN, (m + 1) * OWN)
        cot = dot(hit[at], cot_ref[m, 0]).astype(BF)
        for z in range(NZ):
            out_ref[z, at, :HALF] = cot
            out_ref[z, at, HALF:] = code[at]


def project(side_ref, mine_ref, got_ref, proj_ref, out_ref):
    pooled = jnp.where(lax.axis_index("pipe") == 1, mine_ref[...], got_ref[...])
    live = wide(side_ref[0, :, HALF:], HALF // 128) >= 0
    feat = jnp.where(live, dot(pooled, proj_ref[...]), 0.0).astype(BF)
    for z in range(NZ):
        out_ref[z, :, :HALF] = feat
        out_ref[z, :, HALF:] = pooled[:, z * SLICE : (z + 1) * SLICE]


def mix(spread_ref, w, part_ref, send_ref):
    mine, other = halves()
    send_ref[...] = dot(spread_ref[...], w[:, other]).astype(BF)
    part_ref[...] = dot(spread_ref[...], w[:, mine])


def unmix(slope_ref, got_ref, point_ref, layer):
    mine, other = halves()
    own = dot_nt(slope_ref[...], point_ref[layer, :, mine])
    return own + dot_nt(got_ref[...], point_ref[layer, :, other])


def layer0(slots_ref, depth_ref, near_ref, point_ref, spread_ref, part_ref, send_ref,
           stack, w, sem):
    copy = pltpu.make_async_copy(point_ref.at[0], w, sem)
    copy.start()
    for rows in chunks():
        put_weighed(stack, rows, slots_ref[rows, :HALF].astype(F32), depth_ref, 0, False)
    spread_ref[...] = dot(near_ref[...], stack[...]).astype(BF)
    copy.wait()
    mix(spread_ref, w, part_ref, send_ref)


def layer1(slots_ref, side_ref, part_ref, got_ref, depth_ref, bias_ref, far_ref, point_ref,
           pre_ref, grid_ref, spread_ref, part_out_ref, send_ref, stack, w, sem):
    copy = pltpu.make_async_copy(point_ref.at[1], w, sem)
    copy.start()
    for rows in chunks():
        pre = part_ref[rows] + got_ref[rows].astype(F32) + bias_ref[0:1]
        pre_ref[rows] = pre
        value = slots_ref[rows, :HALF].astype(F32) + gelu_parts(pre)[0]
        grid = jnp.where(live_at(side_ref, rows), value, 0.0).astype(BF)
        grid_ref[rows] = grid
        put_weighed(stack, rows, grid.astype(F32), depth_ref, 1, False)
    spread_ref[...] = dot(far_ref[...], stack[...]).astype(BF)
    copy.wait()
    mix(spread_ref, w, part_out_ref, send_ref)


def head(side_ref, part_ref, got_ref, grid_ref, bias_ref,
         mixed_ref, slope_ref, sum_ref, mixed, sem):
    for m in range(MB):
        at = pl.ds(pl.multiple_of(lax.axis_index("z") * ROWS + m * OWN, OWN), OWN)
        pre = part_ref[at] + got_ref[at].astype(F32) + bias_ref[1:2]
        rows = (grid_ref[at].astype(F32) + gelu_parts(pre)[0]).astype(BF)
        code = wide(side_ref[at, HALF:], 2).astype(jnp.int32)
        hit = jnp.where(code == iota((OWN, CELLS), 1), 1.0, 0.0).astype(BF)
        mixed[m, 0] = dot_tn(hit, rows).astype(BF)
    out = pltpu.make_async_copy(mixed, mixed_ref, sem)
    out.start()
    total = None
    for rows in chunks():
        pre = part_ref[rows] + got_ref[rows].astype(F32) + bias_ref[1:2]
        slope = side_ref[rows, :HALF].astype(F32) * gelu_parts(pre)[1]
        slope = jnp.where(live_at(side_ref, rows), slope, 0.0)
        slope_ref[rows] = slope.astype(BF)
        total = slope if total is None else total + slope
    sum_ref[...] = jnp.sum(total, axis=0, keepdims=True)
    out.wait()


def back1(side_ref, slope_ref, got_ref, grid_ref, pre_ref, sum_ref, depth_ref, far_ref,
          far_long_ref, point_ref, masked_ref, out_ref, grads_ref, stack, moved, grad):
    grad[...] = unmix(slope_ref, got_ref, point_ref, 1)
    for rows in chunks():
        put_weighed(stack, rows, grad[rows], depth_ref, 1, True)
    grads_ref[...] = jnp.zeros((16, HALF), F32)
    depth_rows(far_long_ref, grid_ref[...], grad, moved, grads_ref, list(range(9)))
    grad[...] = dot(far_ref[...], stack[...])
    total = None
    for rows in chunks():
        masked = side_ref[rows, :HALF].astype(F32) + grad[rows]
        masked = jnp.where(live_at(side_ref, rows), masked, 0.0)
        masked_ref[rows] = masked
        slope = masked * gelu_parts(pre_ref[rows])[1]
        out_ref[rows] = slope.astype(BF)
        total = slope if total is None else total + slope
    grads_ref[9:10] = sum_ref[...]
    grads_ref[10:11] = jnp.sum(total, axis=0, keepdims=True)


def slope_rows(side, values):
    row = iota((256, 1), 0)
    group, i = row >> 4, row & 15
    column = lax.axis_index("z") * 192 + group * COLS + i - side * HALF
    column = jnp.where(i < COLS, column, -1)
    picker = jnp.where(iota((256, HALF), 1) == column, 1.0, 0.0).astype(BF)
    return [dot_nt(picker, value) for value in values]


def back0(slots_ref, side_ref, slope_ref, got_ref, slope1_ref, got1_ref, spread0_ref, spread1_ref,
          masked_ref, grads_ref, depth_ref, near_ref, near_long_ref, point_ref, out_ref,
          stack, moved, grad, grads):
    p = lax.axis_index("pipe")
    own = slope_rows(p, (slope_ref[...], slope1_ref[...]))
    far = slope_rows(1 - p, (got_ref[...], got1_ref[...]))
    point0 = dot((own[0] + far[0]).astype(BF), spread0_ref[...])
    point1 = dot((own[1] + far[1]).astype(BF), spread1_ref[...]).astype(BF)
    for g in range(PLANE):
        out_ref[g, 16:32] = point1[16 * g : 16 * g + 16]
    grad[...] = unmix(slope_ref, got_ref, point_ref, 0)
    for rows in chunks():
        put_weighed(stack, rows, grad[rows], depth_ref, 0, True)
    grads[0:16] = grads_ref[...]
    grads[16:32] = jnp.zeros((16, HALF), F32)
    where = [11 + t if t < 5 else 23 + t for t in range(9)]
    depth_rows(near_long_ref, slots_ref[:, :HALF], grad, moved, grads, where)
    tail, last = grads[16:32], grads[0:16].astype(BF)
    for g in range(PLANE):
        out_ref[g, 0:16] = (point0[16 * g : 16 * g + 16] + tail).astype(BF)
        out_ref[g, 48:64] = last
    grad[...] = dot(near_ref[...], stack[...])
    for rows in chunks():
        tile_grad = jnp.where(live_at(side_ref, rows), masked_ref[rows] + grad[rows], 0.0)
        stack[rows] = tile_grad.astype(BF)
    proj = dot_tn(slots_ref[:, HALF:], stack[0:ALL]).astype(BF)
    for g in range(PLANE):
        out_ref[g, 32:48] = proj[16 * g : 16 * g + 16]


def finish(in_ref, proj_ref, point_ref, depth_ref, bias_ref):
    sums = []
    for r in range(0, 64, 16):
        total = in_ref[0, r : r + 16].astype(F32)
        for g in range(1, PLANE):
            total = total + in_ref[g, r : r + 16].astype(F32)
        sums.append(total)
    proj_ref[...] = sums[2]
    for layer in range(2):
        for i in range(COLS):
            point_ref[i, layer : layer + 1] = sums[layer][i : i + 1]
    for t in range(9):
        depth_ref[t, 0:1] = sums[3][11 + t : 12 + t] if t < 5 else sums[0][7 + t : 8 + t]
        depth_ref[t, 1:2] = sums[3][t : t + 1]
    bias_ref[1:2] = sums[3][9:10]
    bias_ref[0:1] = sums[3][10:11]


def call(body, outs, specs, *args, scratch=(), out_specs=None, mib=20):
    return pl.pallas_call(
        body, out_shape=[jax.ShapeDtypeStruct(s, d) for s, d in outs], in_specs=specs,
        out_specs=out_specs or [VM] * len(outs), scratch_shapes=list(scratch),
        compiler_params=pltpu.CompilerParams(vmem_limit_bytes=mib * 1024 * 1024),
        name=body.__name__)(*args)


def swap(value):
    return lax.ppermute(value, "pipe", [(0, 1), (1, 0)])


def shards(tiles, counts, cells, block_in, block_out, proj, depth, point, bias, cotangent):
    depth = depth.transpose(1, 0, 2)
    x = tiles.reshape(ROWS * POS, CH)
    (x,) = call(
        first_section, [(x.shape, BF)], [HB] * 3, x, block_in, block_out, mib=60,
        scratch=[pltpu.VMEM(x.shape, BF), pltpu.VMEM((CH, 512), BF), pltpu.VMEM((512, CH), BF),
                 pltpu.SemaphoreType.DMA((3, 4))])
    x = lax.ppermute(x, "pipe", [(0, 1)])
    (own_side,) = call(side_rows, [((NZ, ROWS, SIDE), BF)], [SM, SM, VM], cells, counts, cotangent)
    side = lax.all_to_all(own_side, "z", 0, 0, tiled=True).reshape(ALL, SIDE)
    (mine,) = call(second_section, [((ROWS, CH), BF)], [VM, HB, HB], x, block_in, block_out,
                   scratch=[pltpu.VMEM((CH, 512), BF), pltpu.VMEM((512, CH), BF),
                            pltpu.SemaphoreType.DMA((2, 2))], mib=52)
    got = lax.ppermute(mine, "pipe", [(1, 0)])
    (slots,) = call(project, [((NZ, ROWS, WIDTH), BF)], [VM] * 4, own_side, mine, got, proj)
    slots = lax.all_to_all(slots, "z", 0, 0, tiled=True).reshape(ALL, WIDTH)
    half_b, half_f = ((ALL, HALF), BF), ((ALL, HALF), F32)
    hits, long_hits = ((ALL, 9 * ALL), BF), ((9 * ALL, ALL), BF)
    near, near_long, far, far_long = call(
        taps, [hits, long_hits, hits, long_hits], [VM], side)
    stack = pltpu.VMEM((9 * ALL, HALF), BF)
    moved, grad = pltpu.VMEM((9 * ALL, HALF), F32), pltpu.VMEM((ALL, HALF), F32)
    sem = pltpu.SemaphoreType.DMA
    spread0, part, send = call(
        layer0, [half_b, half_f, half_b], [VM] * 3 + [HB], slots, depth, near,
        point, scratch=[stack, pltpu.VMEM((HALF, FEAT), BF), sem], mib=48)
    pre0, grid1, spread1, part, send = call(
        layer1, [half_f, half_b, half_b, half_f, half_b], [VM] * 7 + [HB],
        slots, side, part, swap(send), depth, bias, far, point,
        scratch=[stack, pltpu.VMEM((HALF, FEAT), BF), sem], mib=48)
    mixed, slope1, sum1 = call(
        head, [((MB, 1, CELLS, HALF), BF), half_b, ((1, HALF), F32)], [VM] * 5,
        side, part, swap(send), grid1, bias, out_specs=[HB, VM, VM],
        scratch=[pltpu.VMEM((MB, 1, CELLS, HALF), BF), sem])
    got1 = swap(slope1)
    masked, slope0, grads = call(
        back1, [half_f, half_b, ((16, HALF), F32)], [VM] * 10,
        side, slope1, got1, grid1, pre0, sum1, depth, far, far_long, point,
        scratch=[stack, moved, grad])
    (sums,) = call(
        back0, [((PLANE, 64, HALF), BF)], [VM] * 14,
        slots, side, slope0, swap(slope0), slope1, got1, spread0, spread1, masked, grads, depth,
        near, near_long, point,
        scratch=[stack, moved, grad, pltpu.VMEM((32, HALF), F32)])
    sums = lax.all_to_all(sums, ("y", "x"), 0, 0, tiled=True)
    grad_proj, grad_point, grad_depth, grad_bias = call(
        finish, [((16, HALF), F32), ((COLS, 2, HALF), F32), ((9, 2, HALF), F32), ((2, HALF), F32)],
        [VM], sums)
    return (mixed, grad_proj, grad_point.transpose(1, 2, 0), grad_depth.transpose(1, 0, 2), grad_bias)


def solution(mesh):
    grid = Mesh(mesh.devices.reshape(2, NZ, NY, NX), ("pipe", "z", "y", "x"))
    dp = ("z", "y", "x")
    in_specs = (
        P(None, dp, None, None, None),
        P(None, dp),
        P(None, dp, None),
        P("pipe", None, None),
        P("pipe", None, None),
        P(None, "pipe"),
        P(None, None, "pipe"),
        P(None, "pipe", None),
        P(None, "pipe"),
        P(None, dp, None, "pipe"),
    )
    out_specs = (
        P(None, dp, None, "pipe"),
        P(dp, "pipe"),
        P(None, "pipe", dp),
        P(None, None, "pipe"),
        P(None, "pipe"),
    )
    return jax.shard_map(shards, mesh=grid, in_specs=in_specs, out_specs=out_specs, check_vma=False)
```

time: 1290 us -> 107 us (0.08)
  waiting for transfers between devices: 588 us -> 22.9 us
  blocking collectives: 581 us -> 28.5 us
  matrix products: 47.2 us -> 0 us
  Pallas kernels: 0 us -> 29.6 us
  other arithmetic: 27.7 us -> 0.01 us
  starting transfers between devices: 3.03 us -> 22.3 us
  local copies, waits for them, and re-layouts: 20.8 us -> 2.17 us
  between operations: 15.5 us -> 0.81 us
    psum x1 -> x0, blocking collectives: 581 us -> none  [shards(): lax.psum((jnp.stack(depth_grads), jnp.stack(bias_grads)), 'dp')]
    reduce_scatter x3 -> x0, waiting for transfers between devices: 522 us -> none  [the longest x1 491 us: shards(): lax.psum_scatter(proj_grad, 'dp', scatter_dimension=0, tiled=True)]
    dot_general x12 -> x0, matrix products: 47.2 us -> none  [the longest x3 12.9 us: encode_block(): jnp.dot(hidden, w_out, preferred_element_type=jnp.float32)]
    psum x1 -> x0, waiting for transfers between devices: 30.5 us -> none  [broadcast(): return lax.psum(block, axis)]
    pallas_call x0 -> x11, Pallas kernels: none -> 29.6 us  [call(): pl.pallas_call(body, out_shape=[jax.ShapeDtypeStruct(s, d) for s, d in ou...]
    all_to_all x0 -> x1, blocking collectives: none -> 28.5 us  [shards(): sums = lax.all_to_all(sums, ('y', 'x'), 0, 0, tiled=True)]
    all_gather x2 -> x0, waiting for transfers between devices: 27.8 us -> none  [shards(): slope_all = lax.all_gather(slope_half, 'pipe', axis=2, tiled=True)]
    all_to_all x0 -> x2, waiting for transfers between devices: none -> 16.5 us  [the longest x1 12.4 us: shards(): slots = lax.all_to_all(slots, 'z', 0, 0, tiled=True).reshape(ALL, WIDTH)]
  transfers between devices with their start and end apart: 9 -> 8, of which waited for: 8 -> 7; matrix products, arithmetic and copies ran while one was open for 2% -> 0% of each run, Pallas kernels for 0% -> 8%
where the time goes in v2:
time: 107 us; the launch traced here: 106 us
  Pallas kernels  29.6 us (28%)
  blocking collectives  28.5 us (27%)
  waiting for transfers between devices  22.9 us (21%)
  starting transfers between devices  22.3 us (21%)
  local copies, waits for them, and re-layouts  2.17 us (2%)
    pallas_call x11, Pallas kernels, call(): pl.pallas_call(body, out_shape=[jax.ShapeDtypeStruct(s, d) for s, d in ou...  29.6 us
    all_to_all x1, blocking collectives, shards(): sums = lax.all_to_all(sums, ('y', 'x'), 0, 0, tiled=True)  28.5 us
    all_to_all x1, waiting for transfers between devices, shards(): slots = lax.all_to_all(slots, 'z', 0, 0, tiled=True).reshape(ALL, WIDTH)  12.4 us
    all_to_all x1, starting transfers between devices, shards(): side = lax.all_to_all(own_side, 'z', 0, 0, tiled=True).reshape(ALL, SIDE)  9.01 us
    ppermute x4, waiting for transfers between devices, swap(): return lax.ppermute(value, 'pipe', [(0, 1), (1, 0)])  5.4 us
    ppermute x4, starting transfers between devices, swap(): return lax.ppermute(value, 'pipe', [(0, 1), (1, 0)])  4.96 us
    all_to_all x1, waiting for transfers between devices, shards(): side = lax.all_to_all(own_side, 'z', 0, 0, tiled=True).reshape(ALL, SIDE)  4.12 us
    ppermute x1, starting transfers between devices, shards(): got = lax.ppermute(mine, 'pipe', [(1, 0)])  3.51 us
  transfers between devices with their start and end apart: 8, of which 7 were waited for; matrix products, arithmetic and copies ran while one was open for 0% of the time, Pallas kernels for 8%

profile of v2, /device:TPU:1, one launch (start us, length us, event | category | flops | bytes accessed | tf_op | source)
XLA Modules:
  0.0 106.2 jit_solution(17656248390382147782)
XLA Ops:
  0.7 4.6 %first_section.1 = bf16[256,2048]{1,0:T(8,128)(2,1)} custom-call(bf16[256,2048]{1,0:T(8,128)(2,1)} %bitcast.20, bf16[1,2048,512]{2,1,0:T(8,128)(2,1)} %w_in_hbm.3, bf16[1,512,2048]{2,1,0:T(8,128)(2,1)} %w_out_hbm.3), custom_call_target="tpu_custom_call" | custom-call | tf_op jit(solution)/shard_map/first_section/pallas_call | solution.py:339
  5.2 1.3 %collective-permute-start = (bf16[256,2048]{1,0:T(8,128)(2,1)}, bf16[256,2048]{1,0:T(8,128)(2,1)S(1)}, u32[]{:S(2)}, u32[]{:S(2)}) collective-permute-start(bf16[256,2048]{1,0:T(8,128)(2,1)} %first_section.1), channel_id=1, source_target_pairs={{0,128},{1,129},{2,130},{3,131},{4,132},{5,133},{6,134},{7,135},{8... | collective-permute-start | bytes 3145736 | tf_op jit(solution)/shard_map/ppermute | solution.py:357
  6.7 1.6 %side_rows.1.side_ref = bf16[8,32,896]{2,1,0:T(8,128)(2,1)} custom-call(s32[2,1,16]{2,1,0:T(1,128)S(1)} %copy-done.8, s32[2,1]{1,0:T(2,128)S(1)} %copy.15.counts_ref, bf16[2,1,256,768]{3,2,1,0:T(8,128)(2,1)S(1)} %copy-done.6), custom_call_target="tpu_custom_call" | custom-call | tf_op jit(solution)/shard_map/side_rows/pallas_call | solution.py:339
  8.2 9.0 %all-to-all-start = ((bf16[8,32,896]{2,1,0:T(8,128)(2,1)}), bf16[8,32,896]{2,1,0:T(8,128)(2,1)S(1)}, u32[]{:S(2)}, u32[]{:S(2)}) async-start(bf16[8,32,896]{2,1,0:T(8,128)(2,1)} %side_rows.1.side_ref), calls=%async_computation | async-start | bytes 917504 | tf_op jit(solution)/shard_map/all_to_all | solution.py:359
  17.2 3.6 %second_section.1.mine_ref = bf16[32,2048]{1,0:T(8,128)(2,1)S(1)} custom-call(bf16[256,2048]{1,0:T(8,128)(2,1)S(1)} %collective-permute-done.x_ref, bf16[1,2048,512]{2,1,0:T(8,128)(2,1)} %w_in_hbm.3, bf16[1,512,2048]{2,1,0:T(8,128)(2,1)} %w_out_hbm.3), custom_call_target="tpu_custom_call" | custom-call | tf_op jit(solution)/shard_map/second_section/pallas_call | solution.py:339
  20.8 3.5 %collective-permute-start.1 = (bf16[32,2048]{1,0:T(8,128)(2,1)S(1)}, bf16[32,2048]{1,0:T(8,128)(2,1)S(1)}, u32[]{:S(2)}, u32[]{:S(2)}) collective-permute-start(bf16[32,2048]{1,0:T(8,128)(2,1)S(1)} %second_section.1.mine_ref), channel_id=1, source_target_pairs={{128,0},{129,1},{130,2},{131,3},{132,4},{133,5},{134,6},{135,7},{1... | collective-permute-start | bytes 393224 | tf_op jit(solution)/shard_map/ppermute | solution.py:363
  24.3 1.0 collective-permute-done.1.got_ref
  25.3 2.5 %project.1 = bf16[8,32,1024]{2,1,0:T(8,128)(2,1)} custom-call(bf16[8,32,896]{2,1,0:T(8,128)(2,1)} %side_rows.1.side_ref, bf16[32,2048]{1,0:T(8,128)(2,1)S(1)} %second_section.1.mine_ref, bf16[32,2048]{1,0:T(8,128)(2,1)S(1)} %collective-permute-done.1.got_ref, bf16[2048,768]{1,0:T(8,128)(2,1)S(1)} %copy-done), custom_call_target="tpu_custom_call" | custom-call | tf_op jit(solution)/shard_map/project/pallas_call | solution.py:339
  27.8 4.1 %all-to-all-done = bf16[8,32,896]{2,1,0:T(8,128)(2,1)S(1)} async-done(((bf16[8,32,896]{2,1,0:T(8,128)(2,1)}), bf16[8,32,896]{2,1,0:T(8,128)(2,1)S(1)}, u32[]{:S(2)}, u32[]{:S(2)}) %all-to-all-start) | async-done | bytes 458784 | tf_op jit(solution)/shard_map/all_to_all | solution.py:359
  31.9 3.5 %all-to-all-start.1 = ((bf16[8,32,1024]{2,1,0:T(8,128)(2,1)}), bf16[8,32,1024]{2,1,0:T(8,128)(2,1)S(1)}, u32[]{:S(2)}, u32[]{:S(2)}) async-start(bf16[8,32,1024]{2,1,0:T(8,128)(2,1)} %project.1), calls=%async_computation.1 | async-start | bytes 1048576 | tf_op jit(solution)/shard_map/all_to_all | solution.py:365
  36.1 1.0 copy-done.1
  37.1 1.0 copy-done.3
  38.1 12.4 %all-to-all-done.1 = bf16[8,32,1024]{2,1,0:T(8,128)(2,1)S(1)} async-done(((bf16[8,32,1024]{2,1,0:T(8,128)(2,1)}), bf16[8,32,1024]{2,1,0:T(8,128)(2,1)S(1)}, u32[]{:S(2)}, u32[]{:S(2)}) %all-to-all-start.1) | async-done | bytes 524320 | tf_op jit(solution)/shard_map/all_to_all | solution.py:365
  50.5 2.7 %layer0.1 = (bf16[256,768]{1,0:T(8,128)(2,1)S(1)}, f32[256,768]{1,0:T(8,128)S(1)}, bf16[256,768]{1,0:T(8,128)(2,1)S(1)}) custom-call(bf16[256,1024]{1,0:T(8,128)(2,1)S(1)} %bitcast.13, f32[9,2,768]{2,1,0:T(2,128)S(1)} %bitcast.16, bf16[256,2304]{1,0:T(8,128)(2,1)S(1)} %get-tuple-element.27.near_ref, bf16[2,768,1536]{2,1,0:T(8,128)(2,1)} %point_ref.7), custom_call_target="tpu_custom_call" | custom-call | tf_op jit(solution)/shard_map/layer0/pallas_call | solution.py:339
  53.1 3.4 %collective-permute-start.2 = (bf16[256,768]{1,0:T(8,128)(2,1)S(1)}, bf16[256,768]{1,0:T(8,128)(2,1)S(1)}, u32[]{:S(2)}, u32[]{:S(2)}) collective-permute-start(bf16[256,768]{1,0:T(8,128)(2,1)S(1)} %get-tuple-element.29), channel_id=1, source_target_pairs={{0,128},{128,0},{1,129},{129,1},{2,130},{130,2},{3,131},{131,3},{4... | collective-permute-start | bytes 1179656 | tf_op jit(solution)/shard_map/ppermute | solution.py:347
  56.5 1.3 %collective-permute-done.2.got_ref = bf16[256,768]{1,0:T(8,128)(2,1)S(1)} collective-permute-done((bf16[256,768]{1,0:T(8,128)(2,1)S(1)}, bf16[256,768]{1,0:T(8,128)(2,1)S(1)}, u32[]{:S(2)}, u32[]{:S(2)}) %collective-permute-start.2) | collective-permute-done | bytes 393248 | tf_op jit(solution)/shard_map/ppermute | solution.py:347
  57.9 4.1 %layer1.1 = (f32[256,768]{1,0:T(8,128)S(1)}, bf16[256,768]{1,0:T(8,128)(2,1)S(1)}, bf16[256,768]{1,0:T(8,128)(2,1)S(1)}, f32[256,768]{1,0:T(8,128)S(1)}, bf16[256,768]{1,0:T(8,128)(2,1)S(1)}) custom-call(bf16[256,1024]{1,0:T(8,128)(2,1)S(1)} %bitcast.14, bf16[256,896]{1,0:T(8,128)(2,1)S(1)} %bitcast.9, f32[256,768]{1,0:T(8,128)S(1)} %get-tuple-element.28.part_ref, ...), custom_call_target="tpu_custom_call" | custom-call | tf_op jit(solution)/shard_map/layer1/pallas_call | solution.py:339
  62.4 1.3 %collective-permute-done.3.got_ref = bf16[256,768]{1,0:T(8,128)(2,1)S(1)} collective-permute-done((bf16[256,768]{1,0:T(8,128)(2,1)S(1)}, bf16[256,768]{1,0:T(8,128)(2,1)S(1)}, u32[]{:S(2)}, u32[]{:S(2)}) %collective-permute-start.3) | collective-permute-done | bytes 393248 | tf_op jit(solution)/shard_map/ppermute | solution.py:347
  63.8 2.0 %head.1 = (bf16[2,1,256,768]{3,2,1,0:T(8,128)(2,1)}, bf16[256,768]{1,0:T(8,128)(2,1)S(1)}, f32[1,768]{1,0:T(1,128)S(1)}) custom-call(bf16[256,896]{1,0:T(8,128)(2,1)S(1)} %bitcast.10, f32[256,768]{1,0:T(8,128)S(1)} %get-tuple-element.31.part_ref, bf16[256,768]{1,0:T(8,128)(2,1)S(1)} %collective-permute-done.3.got_ref, ...), custom_call_target="tpu_custom_call" | custom-call | tf_op jit(solution)/shard_map/head/pallas_call | solution.py:339
  66.4 1.3 %collective-permute-done.4.got_ref.got1_ref = bf16[256,768]{1,0:T(8,128)(2,1)S(1)} collective-permute-done((bf16[256,768]{1,0:T(8,128)(2,1)S(1)}, bf16[256,768]{1,0:T(8,128)(2,1)S(1)}, u32[]{:S(2)}, u32[]{:S(2)}) %collective-permute-start.4) | collective-permute-done | bytes 393248 | tf_op jit(solution)/shard_map/ppermute | solution.py:347
  67.8 3.0 %back1.1 = (f32[256,768]{1,0:T(8,128)S(1)}, bf16[256,768]{1,0:T(8,128)(2,1)S(1)}, f32[16,768]{1,0:T(8,128)S(1)}) custom-call(bf16[256,896]{1,0:T(8,128)(2,1)S(1)} %bitcast.11, bf16[256,768]{1,0:T(8,128)(2,1)S(1)} %get-tuple-element.35.slope_ref.slope1_ref, bf16[256,768]{1,0:T(8,128)(2,1)S(1)} %collective-permute-done.4.got_ref.got1_ref, ...), custom_call_target="tpu_custom_call" | custom-call | tf_op jit(solution)/shard_map/back1/pallas_call | solution.py:339
  71.2 1.4 %collective-permute-done.5.got_ref = bf16[256,768]{1,0:T(8,128)(2,1)S(1)} collective-permute-done((bf16[256,768]{1,0:T(8,128)(2,1)S(1)}, bf16[256,768]{1,0:T(8,128)(2,1)S(1)}, u32[]{:S(2)}, u32[]{:S(2)}) %collective-permute-start.5) | collective-permute-done | bytes 393248 | tf_op jit(solution)/shard_map/ppermute | solution.py:347
  72.6 4.2 %back0.1 = bf16[16,64,768]{2,1,0:T(8,128)(2,1)S(1)} custom-call(bf16[256,1024]{1,0:T(8,128)(2,1)S(1)} %bitcast.15, bf16[256,896]{1,0:T(8,128)(2,1)S(1)} %bitcast.12, bf16[256,768]{1,0:T(8,128)(2,1)S(1)} %get-tuple-element.39.slope_ref, bf16[256,768]{1,0:T(8,128)(2,1)S(1)} %collective-permute-done.5.got_ref, ...), custom_call_target="tpu_custom_call" | custom-call | tf_op jit(solution)/shard_map/back0/pallas_call | solution.py:339
  76.8 28.5 %all_to_all.15.in_ref = bf16[16,64,768]{2,1,0:T(8,128)(2,1)S(1)} all-to-all(bf16[16,64,768]{2,1,0:T(8,128)(2,1)S(1)} %back0.1), channel_id=1, replica_groups=mesh['pipe'=2,'z'=8,'y'=4,'x'=4] {'y','x'}, dimensions={0} | all-to-all | bytes 3145728 | tf_op jit(solution)/shard_map/all_to_all | solution.py:394
  (30 shorter events, 3.2 us)
Async XLA Ops:
  0.6 5.9 %copy-start.9 = (s32[2,1]{0,1:T(1,128)S(1)}, s32[2,1]{0,1:T(1,128)}, u32[]{:S(2)}) copy-start(s32[2,1]{0,1:T(1,128)} %param.11) | copy-start | bytes 28
  0.6 6.0 %copy-start.6 = (bf16[2,1,256,768]{3,2,1,0:T(8,128)(2,1)S(1)}, bf16[2,1,256,768]{3,2,1,0:T(8,128)(2,1)}, u32[]{:S(2)}) copy-start(bf16[2,1,256,768]{3,2,1,0:T(8,128)(2,1)} %cot_ref.1) | copy-start | bytes 2359300
  0.7 6.0 %copy-start.8 = (s32[2,1,16]{2,1,0:T(1,128)S(1)}, s32[2,1,16]{2,1,0:T(1,128)}, u32[]{:S(2)}) copy-start(s32[2,1,16]{2,1,0:T(1,128)} %cells_ref.1) | copy-start | bytes 388
  5.2 12.0 %collective-permute-start = (bf16[256,2048]{1,0:T(8,128)(2,1)}, bf16[256,2048]{1,0:T(8,128)(2,1)S(1)}, u32[]{:S(2)}, u32[]{:S(2)}) collective-permute-start(bf16[256,2048]{1,0:T(8,128)(2,1)} %first_section.1), channel_id=1, source_target_pairs={{0,128},{1,129},{2,130},{3,131},{4,132},{5,133},{6,134},{7,135},{8... | collective-permute-start | bytes 3145736 | tf_op jit(solution)/shard_map/ppermute | solution.py:357
  8.2 23.7 %all-to-all-start = ((bf16[8,32,896]{2,1,0:T(8,128)(2,1)}), bf16[8,32,896]{2,1,0:T(8,128)(2,1)S(1)}, u32[]{:S(2)}, u32[]{:S(2)}) async-start(bf16[8,32,896]{2,1,0:T(8,128)(2,1)} %side_rows.1.side_ref), calls=%async_computation | async-start | bytes 917504 | tf_op jit(solution)/shard_map/all_to_all | solution.py:359
  17.2 8.1 %copy-start = (bf16[2048,768]{1,0:T(8,128)(2,1)S(1)}, bf16[2048,768]{1,0:T(8,128)(2,1)}, u32[]{:S(2)}) copy-start(bf16[2048,768]{1,0:T(8,128)(2,1)} %proj_ref.1) | copy-start | bytes 9437188
  20.8 29.7 %copy-start.5 = (f32[2,9,768]{2,0,1:T(2,128)S(1)}, f32[2,9,768]{2,0,1:T(2,128)}, u32[]{:S(2)}) copy-start(f32[2,9,768]{2,0,1:T(2,128)} %param.16) | copy-start | bytes 165892
  20.8 4.5 %collective-permute-start.1 = (bf16[32,2048]{1,0:T(8,128)(2,1)S(1)}, bf16[32,2048]{1,0:T(8,128)(2,1)S(1)}, u32[]{:S(2)}, u32[]{:S(2)}) collective-permute-start(bf16[32,2048]{1,0:T(8,128)(2,1)S(1)} %second_section.1.mine_ref), channel_id=1, source_target_pairs={{128,0},{129,1},{130,2},{131,3},{132,4},{133,5},{134,6},{135,7},{1... | collective-permute-start | bytes 393224 | tf_op jit(solution)/shard_map/ppermute | solution.py:363
  31.9 18.5 %all-to-all-start.1 = ((bf16[8,32,1024]{2,1,0:T(8,128)(2,1)}), bf16[8,32,1024]{2,1,0:T(8,128)(2,1)S(1)}, u32[]{:S(2)}, u32[]{:S(2)}) async-start(bf16[8,32,1024]{2,1,0:T(8,128)(2,1)} %project.1), calls=%async_computation.1 | async-start | bytes 1048576 | tf_op jit(solution)/shard_map/all_to_all | solution.py:365
  36.1 1.0 copy-start.1
  37.1 1.0 copy-start.3
  50.5 7.4 %copy-start.7 = (f32[2,768]{1,0:T(2,128)S(1)}, f32[2,768]{1,0:T(2,128)}, u32[]{:S(2)}) copy-start(f32[2,768]{1,0:T(2,128)} %bias_ref.3) | copy-start | bytes 18436
  53.1 4.8 %collective-permute-start.2 = (bf16[256,768]{1,0:T(8,128)(2,1)S(1)}, bf16[256,768]{1,0:T(8,128)(2,1)S(1)}, u32[]{:S(2)}, u32[]{:S(2)}) collective-permute-start(bf16[256,768]{1,0:T(8,128)(2,1)S(1)} %get-tuple-element.29), channel_id=1, source_target_pairs={{0,128},{128,0},{1,129},{129,1},{2,130},{130,2},{3,131},{131,3},{4... | collective-permute-start | bytes 1179656 | tf_op jit(solution)/shard_map/ppermute | solution.py:347
  57.9 9.9 %slice-start = ((s8[4718592]{0:T(1024)(128)(4,1)}), s8[4194304]{0:T(1024)(128)(4,1)S(1)}, s32[]{:S(2)}) async-start(s8[4718592]{0:T(1024)(128)(4,1)} %bitcast.6), calls=%async_computation.3 | async-start | bytes 8388608
  57.9 9.9 %slice-start.1 = ((s8[4718592]{0:T(1024)(128)(4,1)}), s8[524288]{0:T(1024)(128)(4,1)S(1)}, s32[]{:S(2)}) async-start(s8[4718592]{0:T(1024)(128)(4,1)} %bitcast.6), calls=%async_computation.4 | async-start | bytes 1048576
  61.9 5.8 %copy-start.4 = (bf16[2304,256]{1,0:T(8,128)(2,1)S(1)}, bf16[2304,256]{1,0:T(8,128)(2,1)}, u32[]{:S(2)}) copy-start(bf16[2304,256]{1,0:T(8,128)(2,1)} %copy-done.3) | copy-start | bytes 3538948
  62.0 1.8 %collective-permute-start.3 = (bf16[256,768]{1,0:T(8,128)(2,1)S(1)}, bf16[256,768]{1,0:T(8,128)(2,1)S(1)}, u32[]{:S(2)}, u32[]{:S(2)}) collective-permute-start(bf16[256,768]{1,0:T(8,128)(2,1)S(1)} %get-tuple-element.32), channel_id=1, source_target_pairs={{0,128},{128,0},{1,129},{129,1},{2,130},{130,2},{3,131},{131,3},{4... | collective-permute-start | bytes 1179656 | tf_op jit(solution)/shard_map/ppermute | solution.py:347
  65.8 2.0 %collective-permute-start.4 = (bf16[256,768]{1,0:T(8,128)(2,1)S(1)}, bf16[256,768]{1,0:T(8,128)(2,1)S(1)}, u32[]{:S(2)}, u32[]{:S(2)}) collective-permute-start(bf16[256,768]{1,0:T(8,128)(2,1)S(1)} %get-tuple-element.35.slope_ref.slope1_ref), channel_id=1, source_target_pairs={{0,128},{128,0},{1,129},{129,1},{2,130},{130,2},{3,131},{131,3},{4... | collective-permute-start | bytes 1179656 | tf_op jit(solution)/shard_map/ppermute | solution.py:347
  67.8 4.8 %copy-start.2 = (bf16[2304,256]{1,0:T(8,128)(2,1)S(1)}, bf16[2304,256]{1,0:T(8,128)(2,1)}, u32[]{:S(2)}) copy-start(bf16[2304,256]{1,0:T(8,128)(2,1)} %copy-done.1) | copy-start | bytes 3538948
  70.8 1.8 %collective-permute-start.5 = (bf16[256,768]{1,0:T(8,128)(2,1)S(1)}, bf16[256,768]{1,0:T(8,128)(2,1)S(1)}, u32[]{:S(2)}, u32[]{:S(2)}) collective-permute-start(bf16[256,768]{1,0:T(8,128)(2,1)S(1)} %get-tuple-element.39.slope_ref), channel_id=1, source_target_pairs={{0,128},{128,0},{1,129},{129,1},{2,130},{130,2},{3,131},{131,3},{4... | collective-permute-start | bytes 1179656 | tf_op jit(solution)/shard_map/ppermute | solution.py:347

commit v3 on v2

--- a/solution.py
+++ b/solution.py
@@ -90,8 +90,7 @@
         stack[at] = (value * depth_ref[s, layer : layer + 1, :]).astype(BF)
 
 
-def depth_rows(long_ref, grid, grad, moved, out_ref, rows):
-    moved[...] = dot(long_ref[...], grid)
+def depth_rows(grad, moved, out_ref, rows):
     for at in (slice(0, 384), slice(384, HALF)):
         sums = [None] * 9
         for i in range(0, ALL, 8):
@@ -117,9 +116,31 @@
     return jnp.maximum(x.astype(F32) + dot(hidden, w_out_ref[0]), 0.0).astype(BF)
 
 
-def first_section(x_hbm, w_in_hbm, w_out_hbm, out_ref, x_ref, w_in_ref, w_out_ref, sems):
+def side_rows(cells_ref, counts_ref, cot_ref, out_ref, code_ref):
+    rows = iota((ROWS, 128), 0)
+    code = jnp.zeros((ROWS, 128), jnp.int32)
+    for m in range(MB):
+        for j in range(OWN):
+            code = jnp.where(rows == m * OWN + j, cells_ref[m, 0, j], code)
+    code = jnp.where(own_live(counts_ref, 128), code, -1)
+    double = jnp.concatenate([code, code], axis=1)
+    code = code.astype(F32).astype(BF)
+    code_ref[...] = code
+    hit = jnp.where(double == iota((ROWS, CELLS), 1), 1.0, 0.0).astype(BF)
+    for m in range(MB):
+        at = slice(m * OWN, (m + 1) * OWN)
+        cot = dot(hit[at], cot_ref[m, 0]).astype(BF)
+        for z in range(NZ):
+            out_ref[z, at, :HALF] = cot
+            out_ref[z, at, HALF:] = code[at]
+
+
+def first_section(cells_ref, counts_ref, cot_hbm, x_hbm, w_in_hbm, w_out_hbm, out_ref, side_hbm,
+                  code_ref, cot_ref, side_ref, x_ref, w_in_ref, w_out_ref, sems):
     n = 4
     step = CH // n
+    first = pltpu.make_async_copy(cot_hbm, cot_ref, sems.at[3, 0])
+    last = pltpu.make_async_copy(side_ref, side_hbm, sems.at[3, 1])
     copies = []
     for k in range(n):
         at = pl.ds(k * step, step)
@@ -127,9 +148,13 @@
         copies.append(pltpu.make_async_copy(w_in_hbm.at[0, at], w_in_ref.at[at], sems.at[1, k]))
     for k in range(n):
         at = pl.ds(k * step, step)
-        copies.append(pltpu.make_async_copy(w_out_hbm.at[0, :, at], w_out_ref.at[:, at], sems.at[2, k]))
-    for copy in copies:
+        copies.append(
+            pltpu.make_async_copy(w_out_hbm.at[0, :, at], w_out_ref.at[:, at], sems.at[2, k]))
+    for copy in [first] + copies:
         copy.start()
+    first.wait()
+    side_rows(cells_ref, counts_ref, cot_ref, side_ref, code_ref)
+    last.start()
     hidden = None
     for k in range(n):
         at = slice(k * step, (k + 1) * step)
@@ -143,6 +168,7 @@
         copies[2 * n + k].wait()
         total = x_ref[:, at].astype(F32) + dot(hidden, w_out_ref[:, at])
         out_ref[:, at] = jnp.maximum(total, 0.0).astype(BF)
+    last.wait()
 
 
 def second_section(x_ref, w_in_hbm, w_out_hbm, out_ref, w_in_ref, w_out_ref, sems):
@@ -170,31 +196,22 @@
         out_ref[:, at] = dot(pool, jnp.maximum(total, 0.0).astype(BF)).astype(BF)
 
 
-def side_rows(cells_ref, counts_ref, cot_ref, out_ref):
-    rows = iota((ROWS, 128), 0)
-    code = jnp.zeros((ROWS, 128), jnp.int32)
-    for m in range(MB):
-        for j in range(OWN):
-            code = jnp.where(rows == m * OWN + j, cells_ref[m, 0, j], code)
-    code = jnp.where(own_live(counts_ref, 128), code, -1)
-    double = jnp.concatenate([code, code], axis=1)
-    code = code.astype(F32).astype(BF)
-    hit = jnp.where(double == iota((ROWS, CELLS), 1), 1.0, 0.0).astype(BF)
-    for m in range(MB):
-        at = slice(m * OWN, (m + 1) * OWN)
-        cot = dot(hit[at], cot_ref[m, 0]).astype(BF)
-        for z in range(NZ):
-            out_ref[z, at, :HALF] = cot
-            out_ref[z, at, HALF:] = code[at]
-
-
-def project(side_ref, mine_ref, got_ref, proj_ref, out_ref):
+def project(code_ref, mine_ref, got_ref, proj_ref, out_hbm, out_ref, sems):
     pooled = jnp.where(lax.axis_index("pipe") == 1, mine_ref[...], got_ref[...])
-    live = wide(side_ref[0, :, HALF:], HALF // 128) >= 0
+    for z in range(NZ):
+        out_ref[z, :, HALF:] = pooled[:, z * SLICE : (z + 1) * SLICE]
+    copies = []
+    for i, at in enumerate((pl.ds(HALF, SLICE), pl.ds(0, HALF))):
+        copies.append(
+            pltpu.make_async_copy(out_ref.at[:, :, at], out_hbm.at[:, :, at], sems.at[i]))
+    copies[0].start()
+    live = wide(code_ref[...], HALF // 128) >= 0
     feat = jnp.where(live, dot(pooled, proj_ref[...]), 0.0).astype(BF)
     for z in range(NZ):
         out_ref[z, :, :HALF] = feat
-        out_ref[z, :, HALF:] = pooled[:, z * SLICE : (z + 1) * SLICE]
+    copies[1].start()
+    for copy in copies:
+        copy.wait()
 
 
 def mix(spread_ref, w, part_ref, send_ref):
@@ -203,27 +220,27 @@
     part_ref[...] = dot(spread_ref[...], w[:, mine])
 
 
-def unmix(slope_ref, got_ref, point_ref, layer):
+def unmix(slope_ref, got_ref, w):
     mine, other = halves()
-    own = dot_nt(slope_ref[...], point_ref[layer, :, mine])
-    return own + dot_nt(got_ref[...], point_ref[layer, :, other])
-
-
-def layer0(slots_ref, depth_ref, near_ref, point_ref, spread_ref, part_ref, send_ref,
-           stack, w, sem):
-    copy = pltpu.make_async_copy(point_ref.at[0], w, sem)
+    return dot_nt(slope_ref[...], w[:, mine]) + dot_nt(got_ref[...], w[:, other])
+
+
+def layer0(slots_ref, depth_ref, near_ref, point_ref, spread_ref, part_ref, send_ref, next_ref,
+           stack, w, sems):
+    copy = pltpu.make_async_copy(point_ref.at[0], w, sems.at[0])
     copy.start()
+    later = pltpu.make_async_copy(point_ref.at[1], next_ref, sems.at[1])
+    later.start()
     for rows in chunks():
         put_weighed(stack, rows, slots_ref[rows, :HALF].astype(F32), depth_ref, 0, False)
     spread_ref[...] = dot(near_ref[...], stack[...]).astype(BF)
     copy.wait()
     mix(spread_ref, w, part_ref, send_ref)
+    later.wait()
 
 
 def layer1(slots_ref, side_ref, part_ref, got_ref, depth_ref, bias_ref, far_ref, point_ref,
-           pre_ref, grid_ref, spread_ref, part_out_ref, send_ref, stack, w, sem):
-    copy = pltpu.make_async_copy(point_ref.at[1], w, sem)
-    copy.start()
+           pre_ref, grid_ref, spread_ref, part_out_ref, send_ref, stack):
     for rows in chunks():
         pre = part_ref[rows] + got_ref[rows].astype(F32) + bias_ref[0:1]
         pre_ref[rows] = pre
@@ -232,8 +249,7 @@
         grid_ref[rows] = grid
         put_weighed(stack, rows, grid.astype(F32), depth_ref, 1, False)
     spread_ref[...] = dot(far_ref[...], stack[...]).astype(BF)
-    copy.wait()
-    mix(spread_ref, w, part_out_ref, send_ref)
+    mix(spread_ref, point_ref, part_out_ref, send_ref)
 
 
 def head(side_ref, part_ref, got_ref, grid_ref, bias_ref,
@@ -260,11 +276,12 @@
 
 def back1(side_ref, slope_ref, got_ref, grid_ref, pre_ref, sum_ref, depth_ref, far_ref,
           far_long_ref, point_ref, masked_ref, out_ref, grads_ref, stack, moved, grad):
-    grad[...] = unmix(slope_ref, got_ref, point_ref, 1)
+    grad[...] = unmix(slope_ref, got_ref, point_ref)
     for rows in chunks():
         put_weighed(stack, rows, grad[rows], depth_ref, 1, True)
     grads_ref[...] = jnp.zeros((16, HALF), F32)
-    depth_rows(far_long_ref, grid_ref[...], grad, moved, grads_ref, list(range(9)))
+    moved[...] = dot(far_long_ref[...], grid_ref[...])
+    depth_rows(grad, moved, grads_ref, list(range(9)))
     grad[...] = dot(far_ref[...], stack[...])
     total = None
     for rows in chunks():
@@ -289,7 +306,9 @@
 
 def back0(slots_ref, side_ref, slope_ref, got_ref, slope1_ref, got1_ref, spread0_ref, spread1_ref,
           masked_ref, grads_ref, depth_ref, near_ref, near_long_ref, point_ref, out_ref,
-          stack, moved, grad, grads):
+          stack, moved, grad, grads, w, sem):
+    copy = pltpu.make_async_copy(point_ref.at[0], w, sem)
+    copy.start()
     p = lax.axis_index("pipe")
     own = slope_rows(p, (slope_ref[...], slope1_ref[...]))
     far = slope_rows(1 - p, (got_ref[...], got1_ref[...]))
@@ -297,13 +316,15 @@
     point1 = dot((own[1] + far[1]).astype(BF), spread1_ref[...]).astype(BF)
     for g in range(PLANE):
         out_ref[g, 16:32] = point1[16 * g : 16 * g + 16]
-    grad[...] = unmix(slope_ref, got_ref, point_ref, 0)
+    moved[...] = dot(near_long_ref[...], slots_ref[:, :HALF])
+    copy.wait()
+    grad[...] = unmix(slope_ref, got_ref, w)
     for rows in chunks():
         put_weighed(stack, rows, grad[rows], depth_ref, 0, True)
     grads[0:16] = grads_ref[...]
     grads[16:32] = jnp.zeros((16, HALF), F32)
     where = [11 + t if t < 5 else 23 + t for t in range(9)]
-    depth_rows(near_long_ref, slots_ref[:, :HALF], grad, moved, grads, where)
+    depth_rows(grad, moved, grads, where)
     tail, last = grads[16:32], grads[0:16].astype(BF)
     for g in range(PLANE):
         out_ref[g, 0:16] = (point0[16 * g : 16 * g + 16] + tail).astype(BF)
@@ -350,18 +371,22 @@
 def shards(tiles, counts, cells, block_in, block_out, proj, depth, point, bias, cotangent):
     depth = depth.transpose(1, 0, 2)
     x = tiles.reshape(ROWS * POS, CH)
-    (x,) = call(
-        first_section, [(x.shape, BF)], [HB] * 3, x, block_in, block_out, mib=60,
-        scratch=[pltpu.VMEM(x.shape, BF), pltpu.VMEM((CH, 512), BF), pltpu.VMEM((512, CH), BF),
-                 pltpu.SemaphoreType.DMA((3, 4))])
+    x, own_side, code = call(
+        first_section, [(x.shape, BF), ((NZ, ROWS, SIDE), BF), ((ROWS, 128), BF)],
+        [SM, SM] + [HB] * 4, cells, counts, cotangent, x, block_in, block_out, mib=60,
+        out_specs=[VM, HB, VM],
+        scratch=[pltpu.VMEM(cotangent.shape, BF), pltpu.VMEM((NZ, ROWS, SIDE), BF),
+                 pltpu.VMEM(x.shape, BF), pltpu.VMEM((CH, 512), BF), pltpu.VMEM((512, CH), BF),
+                 pltpu.SemaphoreType.DMA((4, 4))])
     x = lax.ppermute(x, "pipe", [(0, 1)])
-    (own_side,) = call(side_rows, [((NZ, ROWS, SIDE), BF)], [SM, SM, VM], cells, counts, cotangent)
     side = lax.all_to_all(own_side, "z", 0, 0, tiled=True).reshape(ALL, SIDE)
     (mine,) = call(second_section, [((ROWS, CH), BF)], [VM, HB, HB], x, block_in, block_out,
                    scratch=[pltpu.VMEM((CH, 512), BF), pltpu.VMEM((512, CH), BF),
                             pltpu.SemaphoreType.DMA((2, 2))], mib=52)
     got = lax.ppermute(mine, "pipe", [(1, 0)])
-    (slots,) = call(project, [((NZ, ROWS, WIDTH), BF)], [VM] * 4, own_side, mine, got, proj)
+    (slots,) = call(
+        project, [((NZ, ROWS, WIDTH), BF)], [VM] * 4, code, mine, got, proj, out_specs=[HB],
+        scratch=[pltpu.VMEM((NZ, ROWS, WIDTH), BF), pltpu.SemaphoreType.DMA((2,))])
     slots = lax.all_to_all(slots, "z", 0, 0, tiled=True).reshape(ALL, WIDTH)
     half_b, half_f = ((ALL, HALF), BF), ((ALL, HALF), F32)
     hits, long_hits = ((ALL, 9 * ALL), BF), ((9 * ALL, ALL), BF)
@@ -370,13 +395,13 @@
     stack = pltpu.VMEM((9 * ALL, HALF), BF)
     moved, grad = pltpu.VMEM((9 * ALL, HALF), F32), pltpu.VMEM((ALL, HALF), F32)
     sem = pltpu.SemaphoreType.DMA
-    spread0, part, send = call(
-        layer0, [half_b, half_f, half_b], [VM] * 3 + [HB], slots, depth, near,
-        point, scratch=[stack, pltpu.VMEM((HALF, FEAT), BF), sem], mib=48)
+    spread0, part, send, point1 = call(
+        layer0, [half_b, half_f, half_b, ((HALF, FEAT), BF)], [VM] * 3 + [HB], slots, depth, near,
+        point, scratch=[stack, pltpu.VMEM((HALF, FEAT), BF), pltpu.SemaphoreType.DMA((2,))],
+        mib=48)
     pre0, grid1, spread1, part, send = call(
-        layer1, [half_f, half_b, half_b, half_f, half_b], [VM] * 7 + [HB],
-        slots, side, part, swap(send), depth, bias, far, point,
-        scratch=[stack, pltpu.VMEM((HALF, FEAT), BF), sem], mib=48)
+        layer1, [half_f, half_b, half_b, half_f, half_b], [VM] * 8,
+        slots, side, part, swap(send), depth, bias, far, point1, scratch=[stack])
     mixed, slope1, sum1 = call(
         head, [((MB, 1, CELLS, HALF), BF), half_b, ((1, HALF), F32)], [VM] * 5,
         side, part, swap(send), grid1, bias, out_specs=[HB, VM, VM],
@@ -384,13 +409,14 @@
     got1 = swap(slope1)
     masked, slope0, grads = call(
         back1, [half_f, half_b, ((16, HALF), F32)], [VM] * 10,
-        side, slope1, got1, grid1, pre0, sum1, depth, far, far_long, point,
+        side, slope1, got1, grid1, pre0, sum1, depth, far, far_long, point1,
         scratch=[stack, moved, grad])
     (sums,) = call(
-        back0, [((PLANE, 64, HALF), BF)], [VM] * 14,
+        back0, [((PLANE, 64, HALF), BF)], [VM] * 13 + [HB],
         slots, side, slope0, swap(slope0), slope1, got1, spread0, spread1, masked, grads, depth,
         near, near_long, point,
-        scratch=[stack, moved, grad, pltpu.VMEM((32, HALF), F32)])
+        scratch=[stack, moved, grad, pltpu.VMEM((32, HALF), F32), pltpu.VMEM((HALF, FEAT), BF), sem],
+        mib=44)
     sums = lax.all_to_all(sums, ("y", "x"), 0, 0, tiled=True)
     grad_proj, grad_point, grad_depth, grad_bias = call(
         finish, [((16, HALF), F32), ((COLS, 2, HALF), F32), ((9, 2, HALF), F32), ((2, HALF), F32)],

time: 107 us -> 109 us (1.019)
  local copies, waits for them, and re-layouts: 2.17 us -> 3.36 us
  waiting for transfers between devices: 22.9 us -> 24 us
    unnamed x25 -> x17, local copies, waits for them, and re-layouts: 2.17 us -> 3.36 us
    all_to_all x1, waiting for transfers between devices: 4.12 us -> 5.29 us  [shards(): side = lax.all_to_all(own_side, 'z', 0, 0, tiled=True).reshape(ALL, SIDE)]
    pallas_call x11 -> x10, Pallas kernels: 29.6 us -> 30.3 us  [call(): pl.pallas_call(body, out_shape=[jax.ShapeDtypeStruct(s, d) for s, d in ou...]
  transfers between devices with their start and end apart: 8 -> 8, of which waited for: 7 -> 7; matrix products, arithmetic and copies ran while one was open for 0% -> 0% of each run, Pallas kernels for 8% -> 5%
where the time goes in v3:
time: 109 us
  Pallas kernels  30.3 us (28%)
  blocking collectives  28.5 us (26%)
  waiting for transfers between devices  24 us (22%)
  starting transfers between devices  22.2 us (20%)
  local copies, waits for them, and re-layouts  3.36 us (3%)
    pallas_call x10, Pallas kernels, call(): pl.pallas_call(body, out_shape=[jax.ShapeDtypeStruct(s, d) for s, d in ou...  30.3 us
    all_to_all x1, blocking collectives, shards(): sums = lax.all_to_all(sums, ('y', 'x'), 0, 0, tiled=True)  28.5 us
    all_to_all x1, waiting for transfers between devices, shards(): slots = lax.all_to_all(slots, 'z', 0, 0, tiled=True).reshape(ALL, WIDTH)  12.4 us
    all_to_all x1, starting transfers between devices, shards(): side = lax.all_to_all(own_side, 'z', 0, 0, tiled=True).reshape(ALL, SIDE)  9.04 us
    ppermute x4, waiting for transfers between devices, swap(): return lax.ppermute(value, 'pipe', [(0, 1), (1, 0)])  5.4 us
    all_to_all x1, waiting for transfers between devices, shards(): side = lax.all_to_all(own_side, 'z', 0, 0, tiled=True).reshape(ALL, SIDE)  5.29 us
    ppermute x4, starting transfers between devices, swap(): return lax.ppermute(value, 'pipe', [(0, 1), (1, 0)])  4.98 us
    all_to_all x1, starting transfers between devices, shards(): slots = lax.all_to_all(slots, 'z', 0, 0, tiled=True).reshape(ALL, WIDTH)  3.49 us
  transfers between devices with their start and end apart: 8, of which 7 were waited for; matrix products, arithmetic and copies ran while one was open for 0% of the time, Pallas kernels for 5%

profile of v3, /device:TPU:1, one launch (start us, length us, event | category | flops | bytes accessed | tf_op | source)
XLA Modules:
  0.0 109.1 jit_solution(7046043000985135382)
XLA Ops:
  0.6 1.3 %copy.15.counts_ref = s32[2,1]{1,0:T(2,128)} copy(s32[2,1]{0,1:T(1,128)} %param.11) | data formatting | bytes 16 | tf_op args[1]
  1.9 5.5 %first_section.1 = (bf16[256,2048]{1,0:T(8,128)(2,1)}, bf16[8,32,896]{2,1,0:T(8,128)(2,1)}, bf16[32,128]{1,0:T(8,128)(2,1)}) custom-call(s32[2,1,16]{2,1,0:T(1,128)} %cells_ref.1, s32[2,1]{1,0:T(2,128)} %copy.15.counts_ref, bf16[2,1,256,768]{3,2,1,0:T(8,128)(2,1)} %cot_hbm.1, bf16[256,2048]{1,0:T(8,128)(2,1)} %bitcast.18, bf16[1,2048,512]{2,1,0:T(8,128)(2,1)} %w_in_hbm.3, ...), custom_call_target="tpu_custom_call" | custom-call | tf_op jit(solution)/shard_map/first_section/pallas_call | solution.py:360
  7.4 1.3 %collective-permute-start = (bf16[256,2048]{1,0:T(8,128)(2,1)}, bf16[256,2048]{1,0:T(8,128)(2,1)S(1)}, u32[]{:S(2)}, u32[]{:S(2)}) collective-permute-start(bf16[256,2048]{1,0:T(8,128)(2,1)} %get-tuple-element.33), channel_id=1, source_target_pairs={{0,128},{1,129},{2,130},{3,131},{4,132},{5,133},{6,134},{7,135},{8... | collective-permute-start | bytes 3145736 | tf_op jit(solution)/shard_map/ppermute | solution.py:381
  8.7 9.0 %all-to-all-start = ((bf16[8,32,896]{2,1,0:T(8,128)(2,1)}), bf16[8,32,896]{2,1,0:T(8,128)(2,1)S(1)}, u32[]{:S(2)}, u32[]{:S(2)}) async-start(bf16[8,32,896]{2,1,0:T(8,128)(2,1)} %get-tuple-element.31), calls=%async_computation | async-start | bytes 917504 | tf_op jit(solution)/shard_map/all_to_all | solution.py:382
  17.8 3.6 %second_section.1.mine_ref = bf16[32,2048]{1,0:T(8,128)(2,1)S(1)} custom-call(bf16[256,2048]{1,0:T(8,128)(2,1)S(1)} %collective-permute-done.x_ref, bf16[1,2048,512]{2,1,0:T(8,128)(2,1)} %w_in_hbm.3, bf16[1,512,2048]{2,1,0:T(8,128)(2,1)} %w_out_hbm.3), custom_call_target="tpu_custom_call" | custom-call | tf_op jit(solution)/shard_map/second_section/pallas_call | solution.py:360
  21.4 3.4 %collective-permute-start.1 = (bf16[32,2048]{1,0:T(8,128)(2,1)S(1)}, bf16[32,2048]{1,0:T(8,128)(2,1)S(1)}, u32[]{:S(2)}, u32[]{:S(2)}) collective-permute-start(bf16[32,2048]{1,0:T(8,128)(2,1)S(1)} %second_section.1.mine_ref), channel_id=1, source_target_pairs={{128,0},{129,1},{130,2},{131,3},{132,4},{133,5},{134,6},{135,7},{1... | collective-permute-start | bytes 393224 | tf_op jit(solution)/shard_map/ppermute | solution.py:386
  24.7 1.0 collective-permute-done.1.got_ref
  25.7 1.4 %project.1 = bf16[8,32,1024]{2,1,0:T(8,128)(2,1)} custom-call(bf16[32,128]{1,0:T(8,128)(2,1)S(1)} %copy-done.7, bf16[32,2048]{1,0:T(8,128)(2,1)S(1)} %second_section.1.mine_ref, bf16[32,2048]{1,0:T(8,128)(2,1)S(1)} %collective-permute-done.1.got_ref, bf16[2048,768]{1,0:T(8,128)(2,1)S(1)} %copy-done), custom_call_target="tpu_custom_call" | custom-call | tf_op jit(solution)/shard_map/project/pallas_call | solution.py:360
  27.2 5.3 %all-to-all-done = bf16[8,32,896]{2,1,0:T(8,128)(2,1)S(1)} async-done(((bf16[8,32,896]{2,1,0:T(8,128)(2,1)}), bf16[8,32,896]{2,1,0:T(8,128)(2,1)S(1)}, u32[]{:S(2)}, u32[]{:S(2)}) %all-to-all-start) | async-done | bytes 458784 | tf_op jit(solution)/shard_map/all_to_all | solution.py:382
  32.5 3.5 %all-to-all-start.1 = ((bf16[8,32,1024]{2,1,0:T(8,128)(2,1)}), bf16[8,32,1024]{2,1,0:T(8,128)(2,1)S(1)}, u32[]{:S(2)}, u32[]{:S(2)}) async-start(bf16[8,32,1024]{2,1,0:T(8,128)(2,1)} %project.1), calls=%async_computation.1 | async-start | bytes 1048576 | tf_op jit(solution)/shard_map/all_to_all | solution.py:390
  36.6 1.0 copy-done.1
  37.6 1.0 copy-done.3
  38.6 12.4 %all-to-all-done.1 = bf16[8,32,1024]{2,1,0:T(8,128)(2,1)S(1)} async-done(((bf16[8,32,1024]{2,1,0:T(8,128)(2,1)}), bf16[8,32,1024]{2,1,0:T(8,128)(2,1)S(1)}, u32[]{:S(2)}, u32[]{:S(2)}) %all-to-all-start.1) | async-done | bytes 524320 | tf_op jit(solution)/shard_map/all_to_all | solution.py:390
  51.0 3.2 %layer0.1 = (bf16[256,768]{1,0:T(8,128)(2,1)S(1)}, f32[256,768]{1,0:T(8,128)S(1)}, bf16[256,768]{1,0:T(8,128)(2,1)S(1)}, bf16[768,1536]{1,0:T(8,128)(2,1)S(1)}) custom-call(bf16[256,1024]{1,0:T(8,128)(2,1)S(1)} %bitcast.11, f32[9,2,768]{2,1,0:T(2,128)S(1)} %bitcast.14, bf16[256,2304]{1,0:T(8,128)(2,1)S(1)} %get-tuple-element.34.near_ref, ...), custom_call_target="tpu_custom_call" | custom-call | tf_op jit(solution)/shard_map/layer0/pallas_call | solution.py:360
  54.3 3.4 %collective-permute-start.2 = (bf16[256,768]{1,0:T(8,128)(2,1)S(1)}, bf16[256,768]{1,0:T(8,128)(2,1)S(1)}, u32[]{:S(2)}, u32[]{:S(2)}) collective-permute-start(bf16[256,768]{1,0:T(8,128)(2,1)S(1)} %get-tuple-element.36), channel_id=1, source_target_pairs={{0,128},{128,0},{1,129},{129,1},{2,130},{130,2},{3,131},{131,3},{4... | collective-permute-start | bytes 1179656 | tf_op jit(solution)/shard_map/ppermute | solution.py:368
  57.7 1.3 %collective-permute-done.2.got_ref = bf16[256,768]{1,0:T(8,128)(2,1)S(1)} collective-permute-done((bf16[256,768]{1,0:T(8,128)(2,1)S(1)}, bf16[256,768]{1,0:T(8,128)(2,1)S(1)}, u32[]{:S(2)}, u32[]{:S(2)}) %collective-permute-start.2) | collective-permute-done | bytes 393248 | tf_op jit(solution)/shard_map/ppermute | solution.py:368
  59.0 2.5 %layer1.1 = (f32[256,768]{1,0:T(8,128)S(1)}, bf16[256,768]{1,0:T(8,128)(2,1)S(1)}, bf16[256,768]{1,0:T(8,128)(2,1)S(1)}, f32[256,768]{1,0:T(8,128)S(1)}, bf16[256,768]{1,0:T(8,128)(2,1)S(1)}) custom-call(bf16[256,1024]{1,0:T(8,128)(2,1)S(1)} %bitcast.12, bf16[256,896]{1,0:T(8,128)(2,1)S(1)} %bitcast.7, f32[256,768]{1,0:T(8,128)S(1)} %get-tuple-element.35.part_ref, ...), custom_call_target="tpu_custom_call" | custom-call | tf_op jit(solution)/shard_map/layer1/pallas_call | solution.py:360
  62.0 1.3 %collective-permute-done.3.got_ref = bf16[256,768]{1,0:T(8,128)(2,1)S(1)} collective-permute-done((bf16[256,768]{1,0:T(8,128)(2,1)S(1)}, bf16[256,768]{1,0:T(8,128)(2,1)S(1)}, u32[]{:S(2)}, u32[]{:S(2)}) %collective-permute-start.3) | collective-permute-done | bytes 393248 | tf_op jit(solution)/shard_map/ppermute | solution.py:368
  63.3 2.0 %head.1 = (bf16[2,1,256,768]{3,2,1,0:T(8,128)(2,1)}, bf16[256,768]{1,0:T(8,128)(2,1)S(1)}, f32[1,768]{1,0:T(1,128)S(1)}) custom-call(bf16[256,896]{1,0:T(8,128)(2,1)S(1)} %bitcast.8, f32[256,768]{1,0:T(8,128)S(1)} %get-tuple-element.39.part_ref, bf16[256,768]{1,0:T(8,128)(2,1)S(1)} %collective-permute-done.3.got_ref, ...), custom_call_target="tpu_custom_call" | custom-call | tf_op jit(solution)/shard_map/head/pallas_call | solution.py:360
  65.9 1.3 %collective-permute-done.4.got_ref.got1_ref = bf16[256,768]{1,0:T(8,128)(2,1)S(1)} collective-permute-done((bf16[256,768]{1,0:T(8,128)(2,1)S(1)}, bf16[256,768]{1,0:T(8,128)(2,1)S(1)}, u32[]{:S(2)}, u32[]{:S(2)}) %collective-permute-start.4) | collective-permute-done | bytes 393248 | tf_op jit(solution)/shard_map/ppermute | solution.py:368
  67.3 3.3 %back1.1 = (f32[256,768]{1,0:T(8,128)S(1)}, bf16[256,768]{1,0:T(8,128)(2,1)S(1)}, f32[16,768]{1,0:T(8,128)S(1)}) custom-call(bf16[256,896]{1,0:T(8,128)(2,1)S(1)} %bitcast.9, bf16[256,768]{1,0:T(8,128)(2,1)S(1)} %get-tuple-element.43.slope_ref.slope1_ref, bf16[256,768]{1,0:T(8,128)(2,1)S(1)} %collective-permute-done.4.got_ref.got1_ref, ...), custom_call_target="tpu_custom_call" | custom-call | tf_op jit(solution)/shard_map/back1/pallas_call | solution.py:360
  71.1 1.4 %collective-permute-done.5.got_ref = bf16[256,768]{1,0:T(8,128)(2,1)S(1)} collective-permute-done((bf16[256,768]{1,0:T(8,128)(2,1)S(1)}, bf16[256,768]{1,0:T(8,128)(2,1)S(1)}, u32[]{:S(2)}, u32[]{:S(2)}) %collective-permute-start.5) | collective-permute-done | bytes 393248 | tf_op jit(solution)/shard_map/ppermute | solution.py:368
  72.4 7.3 %back0.1 = bf16[16,64,768]{2,1,0:T(8,128)(2,1)S(1)} custom-call(bf16[256,1024]{1,0:T(8,128)(2,1)S(1)} %bitcast.13, bf16[256,896]{1,0:T(8,128)(2,1)S(1)} %bitcast.10, bf16[256,768]{1,0:T(8,128)(2,1)S(1)} %get-tuple-element.47.slope_ref, bf16[256,768]{1,0:T(8,128)(2,1)S(1)} %collective-permute-done.5.got_ref, ...), custom_call_target="tpu_custom_call" | custom-call | tf_op jit(solution)/shard_map/back0/pallas_call | solution.py:360
  79.7 28.5 %all_to_all.15.in_ref = bf16[16,64,768]{2,1,0:T(8,128)(2,1)S(1)} all-to-all(bf16[16,64,768]{2,1,0:T(8,128)(2,1)S(1)} %back0.1), channel_id=1, replica_groups=mesh['pipe'=2,'z'=8,'y'=4,'x'=4] {'y','x'}, dimensions={0} | all-to-all | bytes 3145728 | tf_op jit(solution)/shard_map/all_to_all | solution.py:420
  (20 shorter events, 3.1 us)
Async XLA Ops:
  7.4 10.4 %collective-permute-start = (bf16[256,2048]{1,0:T(8,128)(2,1)}, bf16[256,2048]{1,0:T(8,128)(2,1)S(1)}, u32[]{:S(2)}, u32[]{:S(2)}) collective-permute-start(bf16[256,2048]{1,0:T(8,128)(2,1)} %get-tuple-element.33), channel_id=1, source_target_pairs={{0,128},{1,129},{2,130},{3,131},{4,132},{5,133},{6,134},{7,135},{8... | collective-permute-start | bytes 3145736 | tf_op jit(solution)/shard_map/ppermute | solution.py:381
  8.7 23.7 %all-to-all-start = ((bf16[8,32,896]{2,1,0:T(8,128)(2,1)}), bf16[8,32,896]{2,1,0:T(8,128)(2,1)S(1)}, u32[]{:S(2)}, u32[]{:S(2)}) async-start(bf16[8,32,896]{2,1,0:T(8,128)(2,1)} %get-tuple-element.31), calls=%async_computation | async-start | bytes 917504 | tf_op jit(solution)/shard_map/all_to_all | solution.py:382
  17.8 8.0 %copy-start = (bf16[2048,768]{1,0:T(8,128)(2,1)S(1)}, bf16[2048,768]{1,0:T(8,128)(2,1)}, u32[]{:S(2)}) copy-start(bf16[2048,768]{1,0:T(8,128)(2,1)} %proj_ref.1) | copy-start | bytes 9437188
  17.8 8.0 %copy-start.7 = (bf16[32,128]{1,0:T(8,128)(2,1)S(1)}, bf16[32,128]{1,0:T(8,128)(2,1)}, u32[]{:S(2)}) copy-start(bf16[32,128]{1,0:T(8,128)(2,1)} %get-tuple-element.32.code_ref) | copy-start | bytes 24580
  21.4 4.3 %collective-permute-start.1 = (bf16[32,2048]{1,0:T(8,128)(2,1)S(1)}, bf16[32,2048]{1,0:T(8,128)(2,1)S(1)}, u32[]{:S(2)}, u32[]{:S(2)}) collective-permute-start(bf16[32,2048]{1,0:T(8,128)(2,1)S(1)} %second_section.1.mine_ref), channel_id=1, source_target_pairs={{128,0},{129,1},{130,2},{131,3},{132,4},{133,5},{134,6},{135,7},{1... | collective-permute-start | bytes 393224 | tf_op jit(solution)/shard_map/ppermute | solution.py:386
  25.7 25.3 %copy-start.5 = (f32[2,9,768]{2,0,1:T(2,128)S(1)}, f32[2,9,768]{2,0,1:T(2,128)}, u32[]{:S(2)}) copy-start(f32[2,9,768]{2,0,1:T(2,128)} %param.16) | copy-start | bytes 165892
  32.5 18.5 %all-to-all-start.1 = ((bf16[8,32,1024]{2,1,0:T(8,128)(2,1)}), bf16[8,32,1024]{2,1,0:T(8,128)(2,1)S(1)}, u32[]{:S(2)}, u32[]{:S(2)}) async-start(bf16[8,32,1024]{2,1,0:T(8,128)(2,1)} %project.1), calls=%async_computation.1 | async-start | bytes 1048576 | tf_op jit(solution)/shard_map/all_to_all | solution.py:390
  36.6 1.0 copy-start.1
  37.6 1.0 copy-start.3
  51.0 8.0 %copy-start.6 = (f32[2,768]{1,0:T(2,128)S(1)}, f32[2,768]{1,0:T(2,128)}, u32[]{:S(2)}) copy-start(f32[2,768]{1,0:T(2,128)} %bias_ref.3) | copy-start | bytes 18436
  54.3 4.7 %collective-permute-start.2 = (bf16[256,768]{1,0:T(8,128)(2,1)S(1)}, bf16[256,768]{1,0:T(8,128)(2,1)S(1)}, u32[]{:S(2)}, u32[]{:S(2)}) collective-permute-start(bf16[256,768]{1,0:T(8,128)(2,1)S(1)} %get-tuple-element.36), channel_id=1, source_target_pairs={{0,128},{128,0},{1,129},{129,1},{2,130},{130,2},{3,131},{131,3},{4... | collective-permute-start | bytes 1179656 | tf_op jit(solution)/shard_map/ppermute | solution.py:368
  61.5 5.8 %copy-start.4 = (bf16[2304,256]{1,0:T(8,128)(2,1)S(1)}, bf16[2304,256]{1,0:T(8,128)(2,1)}, u32[]{:S(2)}) copy-start(bf16[2304,256]{1,0:T(8,128)(2,1)} %copy-done.3) | copy-start | bytes 3538948
  61.5 1.8 %collective-permute-start.3 = (bf16[256,768]{1,0:T(8,128)(2,1)S(1)}, bf16[256,768]{1,0:T(8,128)(2,1)S(1)}, u32[]{:S(2)}, u32[]{:S(2)}) collective-permute-start(bf16[256,768]{1,0:T(8,128)(2,1)S(1)} %get-tuple-element.40), channel_id=1, source_target_pairs={{0,128},{128,0},{1,129},{129,1},{2,130},{130,2},{3,131},{131,3},{4... | collective-permute-start | bytes 1179656 | tf_op jit(solution)/shard_map/ppermute | solution.py:368
  65.3 2.0 %collective-permute-start.4 = (bf16[256,768]{1,0:T(8,128)(2,1)S(1)}, bf16[256,768]{1,0:T(8,128)(2,1)S(1)}, u32[]{:S(2)}, u32[]{:S(2)}) collective-permute-start(bf16[256,768]{1,0:T(8,128)(2,1)S(1)} %get-tuple-element.43.slope_ref.slope1_ref), channel_id=1, source_target_pairs={{0,128},{128,0},{1,129},{129,1},{2,130},{130,2},{3,131},{131,3},{4... | collective-permute-start | bytes 1179656 | tf_op jit(solution)/shard_map/ppermute | solution.py:368
  67.3 5.1 %copy-start.2 = (bf16[2304,256]{1,0:T(8,128)(2,1)S(1)}, bf16[2304,256]{1,0:T(8,128)(2,1)}, u32[]{:S(2)}) copy-start(bf16[2304,256]{1,0:T(8,128)(2,1)} %copy-done.1) | copy-start | bytes 3538948
  70.6 1.8 %collective-permute-start.5 = (bf16[256,768]{1,0:T(8,128)(2,1)S(1)}, bf16[256,768]{1,0:T(8,128)(2,1)S(1)}, u32[]{:S(2)}, u32[]{:S(2)}) collective-permute-start(bf16[256,768]{1,0:T(8,128)(2,1)S(1)} %get-tuple-element.47.slope_ref), channel_id=1, source_target_pairs={{0,128},{128,0},{1,129},{129,1},{2,130},{130,2},{3,131},{131,3},{4... | collective-permute-start | bytes 1179656 | tf_op jit(solution)/shard_map/ppermute | solution.py:368

commit v4 on v3

--- a/solution.py
+++ b/solution.py
@@ -53,7 +53,7 @@
 
 def own_live(counts_ref, width):
     rows = iota((ROWS, width), 0)
-    return (rows & (OWN - 1)) < jnp.where(rows < OWN, counts_ref[0, 0], counts_ref[1, 0])
+    return (rows & (OWN - 1)) < jnp.where(rows < OWN, counts_ref[0, 0], counts_ref[0, 1])
 
 
 def wide(code, times):
@@ -316,7 +316,6 @@
     point1 = dot((own[1] + far[1]).astype(BF), spread1_ref[...]).astype(BF)
     for g in range(PLANE):
         out_ref[g, 16:32] = point1[16 * g : 16 * g + 16]
-    moved[...] = dot(near_long_ref[...], slots_ref[:, :HALF])
     copy.wait()
     grad[...] = unmix(slope_ref, got_ref, w)
     for rows in chunks():
@@ -324,6 +323,7 @@
     grads[0:16] = grads_ref[...]
     grads[16:32] = jnp.zeros((16, HALF), F32)
     where = [11 + t if t < 5 else 23 + t for t in range(9)]
+    moved[...] = dot(near_long_ref[...], slots_ref[:, :HALF])
     depth_rows(grad, moved, grads, where)
     tail, last = grads[16:32], grads[0:16].astype(BF)
     for g in range(PLANE):
@@ -373,7 +373,7 @@
     x = tiles.reshape(ROWS * POS, CH)
     x, own_side, code = call(
         first_section, [(x.shape, BF), ((NZ, ROWS, SIDE), BF), ((ROWS, 128), BF)],
-        [SM, SM] + [HB] * 4, cells, counts, cotangent, x, block_in, block_out, mib=60,
+        [SM, SM] + [HB] * 4, cells, counts.T, cotangent, x, block_in, block_out, mib=60,
         out_specs=[VM, HB, VM],
         scratch=[pltpu.VMEM(cotangent.shape, BF), pltpu.VMEM((NZ, ROWS, SIDE), BF),
                  pltpu.VMEM(x.shape, BF), pltpu.VMEM((CH, 512), BF), pltpu.VMEM((512, CH), BF),
@@ -416,7 +416,7 @@
         slots, side, slope0, swap(slope0), slope1, got1, spread0, spread1, masked, grads, depth,
         near, near_long, point,
         scratch=[stack, moved, grad, pltpu.VMEM((32, HALF), F32), pltpu.VMEM((HALF, FEAT), BF), sem],
-        mib=44)
+        mib=40)
     sums = lax.all_to_all(sums, ("y", "x"), 0, 0, tiled=True)
     grad_proj, grad_point, grad_depth, grad_bias = call(
         finish, [((16, HALF), F32), ((COLS, 2, HALF), F32), ((9, 2, HALF), F32), ((2, HALF), F32)],

time: 109 us -> 106 us (0.972)
  Pallas kernels: 30.3 us -> 27.8 us
  local copies, waits for them, and re-layouts: 3.36 us -> 2.1 us
    pallas_call x10, Pallas kernels: 30.3 us -> 27.8 us  [call(): pl.pallas_call(body, out_shape=[jax.ShapeDtypeStruct(s, d) for s, d in ou...]
    unnamed x17 -> x20, local copies, waits for them, and re-layouts: 3.36 us -> 2.1 us
where the time goes in v4:
time: 106 us; the launch traced here: 105 us
  blocking collectives  28.5 us (27%)
  Pallas kernels  27.8 us (26%)
  waiting for transfers between devices  24 us (23%)
  starting transfers between devices  22.2 us (21%)
  local copies, waits for them, and re-layouts  2.1 us (2%)
    all_to_all x1, blocking collectives, shards(): sums = lax.all_to_all(sums, ('y', 'x'), 0, 0, tiled=True)  28.5 us
    pallas_call x10, Pallas kernels, call(): pl.pallas_call(body, out_shape=[jax.ShapeDtypeStruct(s, d) for s, d in ou...  27.8 us
    all_to_all x1, waiting for transfers between devices, shards(): slots = lax.all_to_all(slots, 'z', 0, 0, tiled=True).reshape(ALL, WIDTH)  12.3 us
    all_to_all x1, starting transfers between devices, shards(): side = lax.all_to_all(own_side, 'z', 0, 0, tiled=True).reshape(ALL, SIDE)  9.03 us
    ppermute x4, waiting for transfers between devices, swap(): return lax.ppermute(value, 'pipe', [(0, 1), (1, 0)])  5.4 us
    all_to_all x1, waiting for transfers between devices, shards(): side = lax.all_to_all(own_side, 'z', 0, 0, tiled=True).reshape(ALL, SIDE)  5.29 us
    ppermute x4, starting transfers between devices, swap(): return lax.ppermute(value, 'pipe', [(0, 1), (1, 0)])  4.96 us
    all_to_all x1, starting transfers between devices, shards(): slots = lax.all_to_all(slots, 'z', 0, 0, tiled=True).reshape(ALL, WIDTH)  3.49 us
  transfers between devices with their start and end apart: 8, of which 7 were waited for; matrix products, arithmetic and copies ran while one was open for 0% of the time, Pallas kernels for 5%

profile of v4, /device:TPU:1, one launch (start us, length us, event | category | flops | bytes accessed | tf_op | source)
XLA Modules:
  0.0 105.4 jit_solution(885832376132939037)
XLA Ops:
  0.6 5.5 %first_section.1 = (bf16[256,2048]{1,0:T(8,128)(2,1)}, bf16[8,32,896]{2,1,0:T(8,128)(2,1)}, bf16[32,128]{1,0:T(8,128)(2,1)}) custom-call(s32[2,1,16]{2,1,0:T(1,128)} %cells_ref.1, s32[1,2]{1,0:T(1,128)} %bitcast.22, bf16[2,1,256,768]{3,2,1,0:T(8,128)(2,1)} %cot_hbm.1, bf16[256,2048]{1,0:T(8,128)(2,1)} %bitcast.21, bf16[1,2048,512]{2,1,0:T(8,128)(2,1)} %w_in_hbm.3, ...), custom_call_target="tpu_custom_call" | custom-call | tf_op jit(solution)/shard_map/first_section/pallas_call | solution.py:360
  6.1 1.3 %collective-permute-start = (bf16[256,2048]{1,0:T(8,128)(2,1)}, bf16[256,2048]{1,0:T(8,128)(2,1)S(1)}, u32[]{:S(2)}, u32[]{:S(2)}) collective-permute-start(bf16[256,2048]{1,0:T(8,128)(2,1)} %get-tuple-element.33), channel_id=1, source_target_pairs={{0,128},{1,129},{2,130},{3,131},{4,132},{5,133},{6,134},{7,135},{8... | collective-permute-start | bytes 3145736 | tf_op jit(solution)/shard_map/ppermute | solution.py:381
  7.4 9.0 %all-to-all-start = ((bf16[8,32,896]{2,1,0:T(8,128)(2,1)}), bf16[8,32,896]{2,1,0:T(8,128)(2,1)S(1)}, u32[]{:S(2)}, u32[]{:S(2)}) async-start(bf16[8,32,896]{2,1,0:T(8,128)(2,1)} %get-tuple-element.31), calls=%async_computation | async-start | bytes 917504 | tf_op jit(solution)/shard_map/all_to_all | solution.py:382
  16.5 3.6 %second_section.1.mine_ref = bf16[32,2048]{1,0:T(8,128)(2,1)S(1)} custom-call(bf16[256,2048]{1,0:T(8,128)(2,1)S(1)} %collective-permute-done.x_ref, bf16[1,2048,512]{2,1,0:T(8,128)(2,1)} %w_in_hbm.3, bf16[1,512,2048]{2,1,0:T(8,128)(2,1)} %w_out_hbm.3), custom_call_target="tpu_custom_call" | custom-call | tf_op jit(solution)/shard_map/second_section/pallas_call | solution.py:360
  20.1 3.4 %collective-permute-start.1 = (bf16[32,2048]{1,0:T(8,128)(2,1)S(1)}, bf16[32,2048]{1,0:T(8,128)(2,1)S(1)}, u32[]{:S(2)}, u32[]{:S(2)}) collective-permute-start(bf16[32,2048]{1,0:T(8,128)(2,1)S(1)} %second_section.1.mine_ref), channel_id=1, source_target_pairs={{128,0},{129,1},{130,2},{131,3},{132,4},{133,5},{134,6},{135,7},{1... | collective-permute-start | bytes 393224 | tf_op jit(solution)/shard_map/ppermute | solution.py:386
  23.5 1.0 collective-permute-done.1.got_ref
  24.4 1.4 %project.1 = bf16[8,32,1024]{2,1,0:T(8,128)(2,1)} custom-call(bf16[32,128]{1,0:T(8,128)(2,1)S(1)} %copy-done.7, bf16[32,2048]{1,0:T(8,128)(2,1)S(1)} %second_section.1.mine_ref, bf16[32,2048]{1,0:T(8,128)(2,1)S(1)} %collective-permute-done.1.got_ref, bf16[2048,768]{1,0:T(8,128)(2,1)S(1)} %copy-done), custom_call_target="tpu_custom_call" | custom-call | tf_op jit(solution)/shard_map/project/pallas_call | solution.py:360
  25.9 5.3 %all-to-all-done = bf16[8,32,896]{2,1,0:T(8,128)(2,1)S(1)} async-done(((bf16[8,32,896]{2,1,0:T(8,128)(2,1)}), bf16[8,32,896]{2,1,0:T(8,128)(2,1)S(1)}, u32[]{:S(2)}, u32[]{:S(2)}) %all-to-all-start) | async-done | bytes 458784 | tf_op jit(solution)/shard_map/all_to_all | solution.py:382
  31.2 3.5 %all-to-all-start.1 = ((bf16[8,32,1024]{2,1,0:T(8,128)(2,1)}), bf16[8,32,1024]{2,1,0:T(8,128)(2,1)S(1)}, u32[]{:S(2)}, u32[]{:S(2)}) async-start(bf16[8,32,1024]{2,1,0:T(8,128)(2,1)} %project.1), calls=%async_computation.1 | async-start | bytes 1048576 | tf_op jit(solution)/shard_map/all_to_all | solution.py:390
  35.3 1.0 copy-done.1
  36.3 1.0 copy-done.3
  37.4 12.3 %all-to-all-done.1 = bf16[8,32,1024]{2,1,0:T(8,128)(2,1)S(1)} async-done(((bf16[8,32,1024]{2,1,0:T(8,128)(2,1)}), bf16[8,32,1024]{2,1,0:T(8,128)(2,1)S(1)}, u32[]{:S(2)}, u32[]{:S(2)}) %all-to-all-start.1) | async-done | bytes 524320 | tf_op jit(solution)/shard_map/all_to_all | solution.py:390
  49.7 3.2 %layer0.1 = (bf16[256,768]{1,0:T(8,128)(2,1)S(1)}, f32[256,768]{1,0:T(8,128)S(1)}, bf16[256,768]{1,0:T(8,128)(2,1)S(1)}, bf16[768,1536]{1,0:T(8,128)(2,1)S(1)}) custom-call(bf16[256,1024]{1,0:T(8,128)(2,1)S(1)} %bitcast.14, f32[9,2,768]{2,1,0:T(2,128)S(1)} %bitcast.17, bf16[256,2304]{1,0:T(8,128)(2,1)S(1)} %get-tuple-element.34.near_ref, ...), custom_call_target="tpu_custom_call" | custom-call | tf_op jit(solution)/shard_map/layer0/pallas_call | solution.py:360
  53.0 3.4 %collective-permute-start.2 = (bf16[256,768]{1,0:T(8,128)(2,1)S(1)}, bf16[256,768]{1,0:T(8,128)(2,1)S(1)}, u32[]{:S(2)}, u32[]{:S(2)}) collective-permute-start(bf16[256,768]{1,0:T(8,128)(2,1)S(1)} %get-tuple-element.36), channel_id=1, source_target_pairs={{0,128},{128,0},{1,129},{129,1},{2,130},{130,2},{3,131},{131,3},{4... | collective-permute-start | bytes 1179656 | tf_op jit(solution)/shard_map/ppermute | solution.py:368
  56.4 1.3 %collective-permute-done.2.got_ref = bf16[256,768]{1,0:T(8,128)(2,1)S(1)} collective-permute-done((bf16[256,768]{1,0:T(8,128)(2,1)S(1)}, bf16[256,768]{1,0:T(8,128)(2,1)S(1)}, u32[]{:S(2)}, u32[]{:S(2)}) %collective-permute-start.2) | collective-permute-done | bytes 393248 | tf_op jit(solution)/shard_map/ppermute | solution.py:368
  57.7 2.5 %layer1.1 = (f32[256,768]{1,0:T(8,128)S(1)}, bf16[256,768]{1,0:T(8,128)(2,1)S(1)}, bf16[256,768]{1,0:T(8,128)(2,1)S(1)}, f32[256,768]{1,0:T(8,128)S(1)}, bf16[256,768]{1,0:T(8,128)(2,1)S(1)}) custom-call(bf16[256,1024]{1,0:T(8,128)(2,1)S(1)} %bitcast.15, bf16[256,896]{1,0:T(8,128)(2,1)S(1)} %bitcast.10, f32[256,768]{1,0:T(8,128)S(1)} %get-tuple-element.35.part_ref, ...), custom_call_target="tpu_custom_call" | custom-call | tf_op jit(solution)/shard_map/layer1/pallas_call | solution.py:360
  60.7 1.3 %collective-permute-done.3.got_ref = bf16[256,768]{1,0:T(8,128)(2,1)S(1)} collective-permute-done((bf16[256,768]{1,0:T(8,128)(2,1)S(1)}, bf16[256,768]{1,0:T(8,128)(2,1)S(1)}, u32[]{:S(2)}, u32[]{:S(2)}) %collective-permute-start.3) | collective-permute-done | bytes 393248 | tf_op jit(solution)/shard_map/ppermute | solution.py:368
  62.0 2.0 %head.1 = (bf16[2,1,256,768]{3,2,1,0:T(8,128)(2,1)}, bf16[256,768]{1,0:T(8,128)(2,1)S(1)}, f32[1,768]{1,0:T(1,128)S(1)}) custom-call(bf16[256,896]{1,0:T(8,128)(2,1)S(1)} %bitcast.11, f32[256,768]{1,0:T(8,128)S(1)} %get-tuple-element.39.part_ref, bf16[256,768]{1,0:T(8,128)(2,1)S(1)} %collective-permute-done.3.got_ref, ...), custom_call_target="tpu_custom_call" | custom-call | tf_op jit(solution)/shard_map/head/pallas_call | solution.py:360
  64.6 1.3 %collective-permute-done.4.got_ref.got1_ref = bf16[256,768]{1,0:T(8,128)(2,1)S(1)} collective-permute-done((bf16[256,768]{1,0:T(8,128)(2,1)S(1)}, bf16[256,768]{1,0:T(8,128)(2,1)S(1)}, u32[]{:S(2)}, u32[]{:S(2)}) %collective-permute-start.4) | collective-permute-done | bytes 393248 | tf_op jit(solution)/shard_map/ppermute | solution.py:368
  66.0 3.3 %back1.1 = (f32[256,768]{1,0:T(8,128)S(1)}, bf16[256,768]{1,0:T(8,128)(2,1)S(1)}, f32[16,768]{1,0:T(8,128)S(1)}) custom-call(bf16[256,896]{1,0:T(8,128)(2,1)S(1)} %bitcast.12, bf16[256,768]{1,0:T(8,128)(2,1)S(1)} %get-tuple-element.43.slope_ref.slope1_ref, bf16[256,768]{1,0:T(8,128)(2,1)S(1)} %collective-permute-done.4.got_ref.got1_ref, ...), custom_call_target="tpu_custom_call" | custom-call | tf_op jit(solution)/shard_map/back1/pallas_call | solution.py:360
  69.7 1.4 %collective-permute-done.5.got_ref = bf16[256,768]{1,0:T(8,128)(2,1)S(1)} collective-permute-done((bf16[256,768]{1,0:T(8,128)(2,1)S(1)}, bf16[256,768]{1,0:T(8,128)(2,1)S(1)}, u32[]{:S(2)}, u32[]{:S(2)}) %collective-permute-start.5) | collective-permute-done | bytes 393248 | tf_op jit(solution)/shard_map/ppermute | solution.py:368
  71.1 4.9 %back0.1 = bf16[16,64,768]{2,1,0:T(8,128)(2,1)S(1)} custom-call(bf16[256,1024]{1,0:T(8,128)(2,1)S(1)} %bitcast.16, bf16[256,896]{1,0:T(8,128)(2,1)S(1)} %bitcast.13, bf16[256,768]{1,0:T(8,128)(2,1)S(1)} %get-tuple-element.47.slope_ref, bf16[256,768]{1,0:T(8,128)(2,1)S(1)} %collective-permute-done.5.got_ref, ...), custom_call_target="tpu_custom_call" | custom-call | tf_op jit(solution)/shard_map/back0/pallas_call | solution.py:360
  76.0 28.5 %all_to_all.15.in_ref = bf16[16,64,768]{2,1,0:T(8,128)(2,1)S(1)} all-to-all(bf16[16,64,768]{2,1,0:T(8,128)(2,1)S(1)} %back0.1), channel_id=1, replica_groups=mesh['pipe'=2,'z'=8,'y'=4,'x'=4] {'y','x'}, dimensions={0} | all-to-all | bytes 3145728 | tf_op jit(solution)/shard_map/all_to_all | solution.py:420
  104.5 0.9 finish.1
  (24 shorter events, 2.2 us)
Async XLA Ops:
  6.1 10.3 %collective-permute-start = (bf16[256,2048]{1,0:T(8,128)(2,1)}, bf16[256,2048]{1,0:T(8,128)(2,1)S(1)}, u32[]{:S(2)}, u32[]{:S(2)}) collective-permute-start(bf16[256,2048]{1,0:T(8,128)(2,1)} %get-tuple-element.33), channel_id=1, source_target_pairs={{0,128},{1,129},{2,130},{3,131},{4,132},{5,133},{6,134},{7,135},{8... | collective-permute-start | bytes 3145736 | tf_op jit(solution)/shard_map/ppermute | solution.py:381
  7.4 23.7 %all-to-all-start = ((bf16[8,32,896]{2,1,0:T(8,128)(2,1)}), bf16[8,32,896]{2,1,0:T(8,128)(2,1)S(1)}, u32[]{:S(2)}, u32[]{:S(2)}) async-start(bf16[8,32,896]{2,1,0:T(8,128)(2,1)} %get-tuple-element.31), calls=%async_computation | async-start | bytes 917504 | tf_op jit(solution)/shard_map/all_to_all | solution.py:382
  16.5 8.0 %copy-start = (bf16[2048,768]{1,0:T(8,128)(2,1)S(1)}, bf16[2048,768]{1,0:T(8,128)(2,1)}, u32[]{:S(2)}) copy-start(bf16[2048,768]{1,0:T(8,128)(2,1)} %proj_ref.1) | copy-start | bytes 9437188
  16.5 8.0 %copy-start.7 = (bf16[32,128]{1,0:T(8,128)(2,1)S(1)}, bf16[32,128]{1,0:T(8,128)(2,1)}, u32[]{:S(2)}) copy-start(bf16[32,128]{1,0:T(8,128)(2,1)} %get-tuple-element.32.code_ref) | copy-start | bytes 24580
  20.1 4.3 %collective-permute-start.1 = (bf16[32,2048]{1,0:T(8,128)(2,1)S(1)}, bf16[32,2048]{1,0:T(8,128)(2,1)S(1)}, u32[]{:S(2)}, u32[]{:S(2)}) collective-permute-start(bf16[32,2048]{1,0:T(8,128)(2,1)S(1)} %second_section.1.mine_ref), channel_id=1, source_target_pairs={{128,0},{129,1},{130,2},{131,3},{132,4},{133,5},{134,6},{135,7},{1... | collective-permute-start | bytes 393224 | tf_op jit(solution)/shard_map/ppermute | solution.py:386
  24.4 25.3 %copy-start.5 = (f32[2,9,768]{2,0,1:T(2,128)S(1)}, f32[2,9,768]{2,0,1:T(2,128)}, u32[]{:S(2)}) copy-start(f32[2,9,768]{2,0,1:T(2,128)} %param.16) | copy-start | bytes 165892
  31.2 18.5 %all-to-all-start.1 = ((bf16[8,32,1024]{2,1,0:T(8,128)(2,1)}), bf16[8,32,1024]{2,1,0:T(8,128)(2,1)S(1)}, u32[]{:S(2)}, u32[]{:S(2)}) async-start(bf16[8,32,1024]{2,1,0:T(8,128)(2,1)} %project.1), calls=%async_computation.1 | async-start | bytes 1048576 | tf_op jit(solution)/shard_map/all_to_all | solution.py:390
  35.3 1.0 copy-start.1
  36.3 1.0 copy-start.3
  49.7 8.0 %copy-start.6 = (f32[2,768]{1,0:T(2,128)S(1)}, f32[2,768]{1,0:T(2,128)}, u32[]{:S(2)}) copy-start(f32[2,768]{1,0:T(2,128)} %bias_ref.3) | copy-start | bytes 18436
  53.0 4.7 %collective-permute-start.2 = (bf16[256,768]{1,0:T(8,128)(2,1)S(1)}, bf16[256,768]{1,0:T(8,128)(2,1)S(1)}, u32[]{:S(2)}, u32[]{:S(2)}) collective-permute-start(bf16[256,768]{1,0:T(8,128)(2,1)S(1)} %get-tuple-element.36), channel_id=1, source_target_pairs={{0,128},{128,0},{1,129},{129,1},{2,130},{130,2},{3,131},{131,3},{4... | collective-permute-start | bytes 1179656 | tf_op jit(solution)/shard_map/ppermute | solution.py:368
  57.7 13.4 %slice-start = ((s8[4718592]{0:T(1024)(128)(4,1)}), s8[4194304]{0:T(1024)(128)(4,1)S(1)}, s32[]{:S(2)}) async-start(s8[4718592]{0:T(1024)(128)(4,1)} %bitcast.7), calls=%async_computation.3 | async-start | bytes 8388608
  60.2 5.8 %copy-start.4 = (bf16[2304,256]{1,0:T(8,128)(2,1)S(1)}, bf16[2304,256]{1,0:T(8,128)(2,1)}, u32[]{:S(2)}) copy-start(bf16[2304,256]{1,0:T(8,128)(2,1)} %copy-done.3) | copy-start | bytes 3538948
  60.2 1.8 %collective-permute-start.3 = (bf16[256,768]{1,0:T(8,128)(2,1)S(1)}, bf16[256,768]{1,0:T(8,128)(2,1)S(1)}, u32[]{:S(2)}, u32[]{:S(2)}) collective-permute-start(bf16[256,768]{1,0:T(8,128)(2,1)S(1)} %get-tuple-element.40), channel_id=1, source_target_pairs={{0,128},{128,0},{1,129},{129,1},{2,130},{130,2},{3,131},{131,3},{4... | collective-permute-start | bytes 1179656 | tf_op jit(solution)/shard_map/ppermute | solution.py:368
  62.0 9.1 %slice-start.1 = ((s8[4718592]{0:T(1024)(128)(4,1)}), s8[524288]{0:T(1024)(128)(4,1)S(1)}, s32[]{:S(2)}) async-start(s8[4718592]{0:T(1024)(128)(4,1)} %bitcast.7), calls=%async_computation.4 | async-start | bytes 1048576
  64.0 2.0 %collective-permute-start.4 = (bf16[256,768]{1,0:T(8,128)(2,1)S(1)}, bf16[256,768]{1,0:T(8,128)(2,1)S(1)}, u32[]{:S(2)}, u32[]{:S(2)}) collective-permute-start(bf16[256,768]{1,0:T(8,128)(2,1)S(1)} %get-tuple-element.43.slope_ref.slope1_ref), channel_id=1, source_target_pairs={{0,128},{128,0},{1,129},{129,1},{2,130},{130,2},{3,131},{131,3},{4... | collective-permute-start | bytes 1179656 | tf_op jit(solution)/shard_map/ppermute | solution.py:368
  66.0 5.1 %copy-start.2 = (bf16[2304,256]{1,0:T(8,128)(2,1)S(1)}, bf16[2304,256]{1,0:T(8,128)(2,1)}, u32[]{:S(2)}) copy-start(bf16[2304,256]{1,0:T(8,128)(2,1)} %copy-done.1) | copy-start | bytes 3538948
  69.3 1.8 %collective-permute-start.5 = (bf16[256,768]{1,0:T(8,128)(2,1)S(1)}, bf16[256,768]{1,0:T(8,128)(2,1)S(1)}, u32[]{:S(2)}, u32[]{:S(2)}) collective-permute-start(bf16[256,768]{1,0:T(8,128)(2,1)S(1)} %get-tuple-element.47.slope_ref), channel_id=1, source_target_pairs={{0,128},{128,0},{1,129},{129,1},{2,130},{130,2},{3,131},{131,3},{4... | collective-permute-start | bytes 1179656 | tf_op jit(solution)/shard_map/ppermute | solution.py:368
